TPU v7x, 128 devices: a whole 4x4x4 slice. The times are simulated.
128 devices in a mesh: rep: 4 (over y_hi, core), fsdp: 32 (over z, x, y_lo).
Axes of the slice: x: 4, y: 4 (y_hi: 2, y_lo: 2; y = y_hi * 2 + y_lo), z: 4, core: 2. Of those that a mesh axis runs over, the one named last changes fastest.
Arguments:
- activations: bfloat16 [2, 4, 12288, 8192], P(None, 'rep', 'fsdp'), may hold values from -6 to 6
- cotangent: bfloat16 [2, 4, 12288, 512], P(None, 'rep', 'fsdp'), may hold values from -6 to 6
- numerator: float32 [4, 8192, 512], P('rep', 'fsdp'), may hold values from -6 to 6
- weight: float32 [4], P('rep'), may hold values from 0.6 to 1.4
- inbox_num: float32 [4, 8192, 512], P('rep', 'fsdp'), may hold values from -3 to 3
- inbox_wt: float32 [4], P('rep'), may hold values from 0.3 to 0.7
- lengths: int32 [2, 4, 32], P(None, 'rep', 'fsdp'), may hold values from 96 to 384, as said below
- step_index: int32 [2], replicated, may hold values from 0 to 1023
Outputs:
- values: bfloat16 [2, 4, 12288, 512], P(None, 'rep', 'fsdp')
- numerator_out: float32 [4, 8192, 512], P('rep', 'fsdp')
- weight_out: float32 [4], P('rep')
- inbox_num_out: float32 [4, 8192, 512], P('rep', 'fsdp')
- inbox_wt_out: float32 [4], P('rep')
Inputs may be any that keep to these rules, and one draw needn't show every extreme that they name: `lengths`: in each step some device's micro-batch has all 384 rows valid, and some other device's has 96.
All inputs are finite; a program needn't handle non-finite values.
Results may differ from a plain program's by a relative error of at most 0.02.
Values may be sent and summed in bfloat16 or wider, within the bound.
A program may use at most 192 MiB of HBM per device.

v0:
```python
from functools import partial
import math

import jax
import jax.numpy as jnp
from jax import lax
from jax.sharding import PartitionSpec as P

D = 8192
TOK_DEV = 384


def for_sending(array):
    return jax.tree.map(lambda a: a.astype(jnp.bfloat16) if a.dtype == jnp.float32 else a, array)


def shifted(array, axis, by):
    count = lax.axis_size(axis)
    return lax.ppermute(array, axis, [(i, (i + by) % count) for i in range(count)])


def deliver(by_offset, kept, kept_wt):
    return (
        shifted(for_sending(kept), "rep", by_offset).astype(kept.dtype),
        shifted(for_sending(kept_wt), "rep", by_offset).astype(kept_wt.dtype),
    )


def per_device(activations, cotangent, numerator, weight, inbox_num, inbox_wt, lengths, step_index):
    shard_count = lax.axis_size("fsdp")
    replica_count = lax.axis_size("rep")
    offset_bits = replica_count.bit_length() - 1
    inv_root = 1.0 / math.sqrt(D)
    step_rate = 0.5 * math.sqrt(D / (TOK_DEV * shard_count))
    local_rows = activations.shape[2]
    senders = [partial(deliver, 1 << bit_number) for bit_number in range(offset_bits)]
    outputs = []
    for section in range(activations.shape[0]):
        weights_bf = (numerator[0] / weight[0]).astype(jnp.bfloat16)
        valid_mask = (jnp.arange(local_rows, dtype=jnp.int32) < lengths[section, 0, 0]).astype(
            jnp.float32
        )
        token_rows = activations[section, 0]
        upstream = (cotangent[section, 0] * valid_mask[:, None]).astype(jnp.bfloat16)
        product = jnp.dot(
            token_rows,
            lax.all_gather(weights_bf, "fsdp", axis=0, tiled=True),
            preferred_element_type=jnp.float32,
        )
        outputs.append((product * inv_root * valid_mask[:, None]).astype(jnp.bfloat16))
        summed = lax.psum_scatter(
            lax.dot_general(
                token_rows, upstream, (((0,), (0,)), ((), ())), preferred_element_type=jnp.float32
            ).astype(jnp.bfloat16),
            "fsdp",
            scatter_dimension=0,
            tiled=True,
        ).astype(jnp.float32)
        grads = summed * inv_root
        plan = 1.0 + 0.5 * jnp.cos(jnp.pi * step_index[section].astype(jnp.float32) / 1024.0)
        kept = 0.5 * (numerator - step_rate * plan * grads[None])
        kept_wt = 0.5 * weight
        numerator = kept + inbox_num
        weight = kept_wt + inbox_wt
        inbox_num, inbox_wt = lax.switch(step_index[section] % offset_bits, senders, kept, kept_wt)
    values = jnp.stack(outputs)[:, None]
    return (values, numerator, weight, inbox_num, inbox_wt)


def solution(mesh):
    in_specs = (
        P(None, "rep", "fsdp", None),
        P(None, "rep", "fsdp", None),
        P("rep", "fsdp", None),
        P("rep"),
        P("rep", "fsdp", None),
        P("rep"),
        P(None, "rep", "fsdp"),
        P(),
    )
    out_specs = (
        P(None, "rep", "fsdp", None),
        P("rep", "fsdp", None),
        P("rep"),
        P("rep", "fsdp", None),
        P("rep"),
    )
    return jax.shard_map(
        per_device, mesh=mesh, in_specs=in_specs, out_specs=out_specs, check_vma=False
    )
```

profile of v0, /device:TPU:18, one launch (start us, length us, event | category | flops | bytes accessed | tf_op | source)
XLA Modules:
  0.0 851.5 jit_solution(7061119255776671065)
XLA Ops:
  7.2 0.0 reduce-scatter.3.cloned.1.call-start
  7.2 1.4 fusion.61
  8.6 0.6 fusion.56
  9.2 0.0 copy-start
  9.2 10.9 %fusion = bf16[8192,512]{0,1:T(8,128)(2,1)} fusion(bf16[2,1,384,8192]{3,2,1,0:T(8,128)(2,1)} %param.12, f32[384]{0:T(512)S(1)} %fusion.56, bf16[2,1,384,512]{3,2,1,0:T(8,128)(2,1)} %param.13), kind=kOutput, calls=%fused_computation.2 | convolution fusion | flops 3226009600 | bytes 15074816 | tf_op jit(solution)/shard_map/dot_general | solution.py:52
  20.1 0.0 copy-start.1
  20.1 0.0 reduce-scatter.3.cloned.1.call-update
  20.1 0.0 all-gather.5.cloned.1.call-start
  20.9 0.0 copy-done
  20.9 0.7 divide_convert_fusion.1
  21.7 0.0 all-gather.5.cloned.1.call-update
  21.7 0.0 reduce-scatter.5.cloned.1.call-start
  21.7 0.7 fusion.54
  22.4 0.0 copy-done.1
  22.4 9.7 %fusion.1 = bf16[8192,512]{0,1:T(8,128)(2,1)} fusion(bf16[2,1,384,8192]{3,2,1,0:T(8,128)(2,1)} %param.12, f32[384]{0:T(512)S(1)} %fusion.54, bf16[2,1,384,512]{3,2,1,0:T(8,128)(2,1)S(1)} %copy-done.1), kind=kOutput, calls=%fused_computation.3 | convolution fusion | flops 3226009600 | bytes 15075328 | tf_op jit(solution)/shard_map/dot_general | solution.py:52
  32.1 0.0 copy-start.4
  32.1 0.0 copy-start.3
  32.1 0.0 reduce-scatter.5.cloned.1.call-update
  32.1 0.0 all-gather.7.cloned.1.call-start
  32.2 0.2 copy.13
  32.4 0.4 copy-done.4
  32.8 0.6 fusion.60
  34.7 0.0 copy-done.3
  34.7 0.2 copy.14
  34.9 174.7 %reduce-scatter.3.cloned.1.call-done = bf16[256,512]{0,1:T(8,128)(2,1)} async-done(((bf16[8192,512]{0,1:T(8,128)(2,1)}), bf16[256,512]{0,1:T(8,128)(2,1)}) %reduce-scatter.3.cloned.1.call-update) | async-done | bytes 262160 | tf_op jit(solution)/shard_map/reduce_scatter | solution.py:51
  209.6 1.8 divide_convert_fusion
  211.4 0.0 all-gather.7.cloned.1.call-update
  216.0 0.7 fusion.55
  216.7 0.6 fusion.57
  217.3 182.6 %all-gather.5.cloned.1.call-done = bf16[1,8192,512]{2,1,0:T(8,128)(2,1)} async-done(((bf16[1,256,512]{2,1,0:T(8,128)(2,1)}), bf16[1,8192,512]{2,1,0:T(8,128)(2,1)}) %all-gather.5.cloned.1.call-update) | async-done | bytes 8388624 | tf_op jit(solution)/shard_map/all_gather | solution.py:47
  399.9 9.7 %fusion.34 = bf16[1,384,512]{1,2,0:T(8,128)(2,1)S(1)} fusion(bf16[2,1,384,8192]{3,2,1,0:T(8,128)(2,1)} %param.12, bf16[1,8192,512]{2,1,0:T(8,128)(2,1)} %all-gather.5.cloned.1.call-done, f32[384]{0:T(512)S(1)} %fusion.57), kind=kOutput, calls=%fused_computation.20 | convolution fusion | flops 3221618688 | bytes 15074816 | tf_op jit(solution)/shard_map/dot_general | solution.py:45
  409.6 15.8 %conditional.8 = (bf16[1,256,512]{2,1,0:T(8,128)(2,1)}, f32[1]{0:T(128)}) conditional(s32[]{:T(128)} %clamp.6, (f32[1,256,512]{1,2,0:T(8,128)S(1)}, f32[1]{0:T(128)}) %tuple.52, (f32[1,256,512]{1,2,0:T(8,128)S(1)}, f32[1]{0:T(128)}) %tuple.52), branch_computations={%region_2.3_spmd, %region_3.4_spmd} | conditional | flops 2 | bytes 1835124
  409.6 0.1 copy.15
  409.8 0.1 collective-permute-start
  409.9 3.2 collective-permute-start.1
  413.1 11.6 %collective-permute-done.1 = bf16[1]{0:T(256)(128)(2,1)} collective-permute-done((bf16[1]{0:T(256)(128)(2,1)}, bf16[1]{0:T(256)(128)(2,1)}, u32[]{:S(2)}, u32[]{:S(2)}) %collective-permute-start.1) | collective-permute-done | bytes 34 | tf_op jit(solution)/shard_map/cond/branch_0_fun/ppermute | solution.py:19
  425.3 0.0 collective-permute-done
  425.5 1.1 copy.17
  426.6 167.3 %reduce-scatter.5.cloned.1.call-done = bf16[256,512]{0,1:T(8,128)(2,1)} async-done(((bf16[8192,512]{0,1:T(8,128)(2,1)}), bf16[256,512]{0,1:T(8,128)(2,1)}) %reduce-scatter.5.cloned.1.call-update) | async-done | bytes 262160 | tf_op jit(solution)/shard_map/reduce_scatter | solution.py:51
  593.8 1.1 convert_add_fusion
  594.9 1.0 copy.21
  595.9 8.8 %conditional.9 = (f32[1,256,512]{2,1,0:T(8,128)S(1)}, f32[1]{0:T(128)}) conditional(s32[]{:T(128)} %clamp.7, (bf16[1,256,512]{1,2,0:T(8,128)(2,1)S(1)}, f32[1]{0:T(128)}) %tuple.53, (bf16[1,256,512]{1,2,0:T(8,128)(2,1)S(1)}, f32[1]{0:T(128)}) %tuple.53), branch_computations={%region_4.5_spmd, %region_5.6_spmd} | conditional | flops 131074 | bytes 2359412
  595.9 0.1 copy.19
  596.1 0.1 collective-permute-start.6
  596.2 4.8 collective-permute-start.7
  601.0 3.1 collective-permute-done.7
  604.7 0.0 collective-permute-done.6
  604.7 0.1 convert_element_type.185
  604.8 0.0 copy-start.2
  604.8 226.9 %all-gather.7.cloned.1.call-done = bf16[1,8192,512]{1,2,0:T(8,128)(2,1)} async-done(((bf16[1,256,512]{1,2,0:T(8,128)(2,1)}), bf16[1,8192,512]{1,2,0:T(8,128)(2,1)}) %all-gather.7.cloned.1.call-update) | async-done | bytes 8388624 | tf_op jit(solution)/shard_map/all_gather | solution.py:47
  831.7 9.7 %fusion.39 = bf16[1,384,512]{1,2,0:T(8,128)(2,1)S(1)} fusion(bf16[2,1,384,8192]{3,2,1,0:T(8,128)(2,1)} %param.12, bf16[1,8192,512]{1,2,0:T(8,128)(2,1)} %all-gather.7.cloned.1.call-done, f32[384]{0:T(512)S(1)} %fusion.55), kind=kOutput, calls=%fused_computation.21 | convolution fusion | flops 3221618688 | bytes 15074816 | tf_op jit(solution)/shard_map/dot_general | solution.py:45
  841.4 0.0 copy-done.2
  841.4 0.1 maximum_bitcast_fusion
  841.5 1.2 copy.20
Async XLA Ops:
  7.2 202.5 %reduce-scatter.3.cloned.1.call-start = ((), (), s32[]{:S(2)}) async-start(), calls=%async_computation.2 | async-start | bytes 8650752 | tf_op jit(solution)/shard_map/reduce_scatter | solution.py:51
  9.2 11.7 %copy-start = (f32[1,256,512]{2,1,0:T(8,128)S(1)}, f32[1,256,512]{2,1,0:T(8,128)}, u32[]{:S(2)}) copy-start(f32[1,256,512]{2,1,0:T(8,128)} %param.14) | copy-start | bytes 1572868
  20.1 2.3 copy-start.1
  20.1 379.8 %all-gather.5.cloned.1.call-start = ((), (), s32[]{:S(2)}) async-start(), calls=%async_computation.4 | async-start | bytes 8650752 | tf_op jit(solution)/shard_map/all_gather | solution.py:47
  21.7 572.2 %reduce-scatter.5.cloned.1.call-start = ((), (), s32[]{:S(2)}) async-start(), calls=%async_computation.3 | async-start | bytes 8650752 | tf_op jit(solution)/shard_map/reduce_scatter | solution.py:51
  32.1 0.7 copy-start.4
  32.1 2.6 copy-start.3
  32.1 799.6 %all-gather.7.cloned.1.call-start = ((), (), s32[]{:S(2)}) async-start(), calls=%async_computation.5 | async-start | bytes 8650752 | tf_op jit(solution)/shard_map/all_gather | solution.py:47
  409.8 15.5 %collective-permute-start = (bf16[1,256,512]{2,1,0:T(8,128)(2,1)S(1)}, bf16[1,256,512]{2,1,0:T(8,128)(2,1)}, u32[]{:S(2)}, u32[]{:S(2)}) collective-permute-start(bf16[1,256,512]{2,1,0:T(8,128)(2,1)S(1)} %copy.15), channel_id=1, source_target_pairs={{0,32},{32,64},{64,96},{96,0},{1,33},{33,65},{65,97},{97,1},{2,34}... | collective-permute-start | bytes 786440 | tf_op jit(solution)/shard_map/cond/branch_0_fun/ppermute | solution.py:19
  409.9 14.8 %collective-permute-start.1 = (bf16[1]{0:T(256)(128)(2,1)}, bf16[1]{0:T(256)(128)(2,1)}, u32[]{:S(2)}, u32[]{:S(2)}) collective-permute-start(bf16[1]{0:T(256)(128)(2,1)} %convert_element_type.116), channel_id=1, source_target_pairs={{0,32},{32,64},{64,96},{96,0},{1,33},{33,65},{65,97},{97,1},{2,34}... | collective-permute-start | bytes 14 | tf_op jit(solution)/shard_map/cond/branch_0_fun/ppermute | solution.py:19
  596.1 8.6 %collective-permute-start.6 = (bf16[1,256,512]{2,1,0:T(8,128)(2,1)S(1)}, bf16[1,256,512]{2,1,0:T(8,128)(2,1)S(1)}, u32[]{:S(2)}, u32[]{:S(2)}) collective-permute-start(bf16[1,256,512]{2,1,0:T(8,128)(2,1)S(1)} %copy.19), channel_id=1, source_target_pairs={{0,64},{32,96},{64,0},{96,32},{1,65},{33,97},{65,1},{97,33},{2,66}... | collective-permute-start | bytes 786440 | tf_op jit(solution)/shard_map/cond/branch_1_fun/ppermute | solution.py:19
  596.2 7.9 collective-permute-start.7
  604.8 236.6 %copy-start.2 = (f32[1,256,512]{2,1,0:T(8,128)}, f32[1,256,512]{2,1,0:T(8,128)S(1)}, u32[]{:S(2)}) copy-start(f32[1,256,512]{2,1,0:T(8,128)S(1)} %get-tuple-element.83) | copy-start | bytes 1572868
Sparse Core Ops, SparseCore 0:
  20.3 189.3 reduce-scatter.2
  211.8 188.0 all-gather.4
  402.3 191.4 reduce-scatter.4
  595.8 235.8 all-gather.6
where the time goes:
time: 852 us; the launch traced here: 851 us
  waiting for transfers between devices  766 us (90%)
  matrix products  39.9 us (5%)
  between operations  22.8 us (3%)
    all_gather x2, waiting for transfers between devices, per_device(): lax.all_gather(weights_bf, 'fsdp', axis=0, tiled=True)  410 us
    reduce_scatter x2, waiting for transfers between devices, per_device(): lax.psum_scatter(lax.dot_general(token_rows, upstream, (((0,), (0,)), (()...  342 us
    dot_general x2, matrix products, per_device(): lax.dot_general(token_rows, upstream, (((0,), (0,)), ((), ())), preferred...  20.6 us
    dot_general x2, matrix products, per_device(): jnp.dot(token_rows, lax.all_gather(weights_bf, 'fsdp', axis=0, tiled=True...  19.4 us
  transfers between devices with their start and end apart: 8, of which 6 were waited for; matrix products, arithmetic and copies ran while one was open for 3% of the time, Pallas kernels for 0%

commit v1 on v0

v1 whole, which is shorter than its diff:
```python
import functools
import math

import jax
import jax.numpy as jnp
from jax import lax
from jax.experimental import pallas as pl
from jax.experimental.pallas import tpu as pltpu
from jax.sharding import PartitionSpec as P

MESH = pl.DeviceIdType.MESH
BF, F32 = jnp.bfloat16, jnp.float32
D, HV, TOK = 8192, 512, 384
INV_ROOT = 1.0 / math.sqrt(D)
HALF_TOK = TOK // 2
ROUTE = 64
HA = 160
SUB = 1024
ORDER = (
    "UPs.0", "AX.0", "T.0.0", "T.0.1", "T.0.2", "T.0.3", "T.0.4", "T.0.5", "T.0.6", "T.0.7", "UPs.1", "UT.0",
    "AY.0", "AZa.0", "C.0.0", "AZb.0", "AY1.0", "AYa.0", "AZe.0", "AZd.0", "D.0.0", "AZc.0", "C.0.1", "AYb.0",
    "AZg.0", "AZf.0", "D.0.1", "AYc.0", "C.0.2", "V.0.2", "V.0.1", "E.0.0", "T.1.0", "AZh.0", "D.0.2", "Fm.0",
    "T.1.1", "C.0.3", "AZi.0", "AYd.0", "V.0.3", "UT.1", "Fp.0", "E.0.1", "Gp.0", "T.1.2", "D.0.3", "V.0.0", "VR.0",
    "E.0.2", "Gm.0", "T.1.3", "C.1.0", "E.0.3", "T.1.4", "VM.0", "D.1.0", "H.0", "T.1.5", "C.1.1", "E.1.0", "J.0",
    "T.1.6", "D.1.1", "C.1.2", "I.0", "Fp.1", "T.1.7", "E.1.1", "Gp.1", "D.1.2", "Fm.1", "U.0", "AX.1", "E.1.2",
    "Gm.1", "C.1.3", "AY.1", "D.1.3", "H.1", "AY1.1", "AZa.1", "AZb.1", "AYa.1", "AZd.1", "V.1.3", "E.1.3", "J.1",
    "AZe.1", "AZf.1", "AZg.1", "I.1", "AZc.1", "AZh.1", "AYb.1", "U.1", "AZi.1", "V.1.2", "AYc.1", "V.1.1", "AYd.1",
    "V.1.0", "VR.1", "VM.1", "M",
)


def kernel(sc, length, act, cot, num, inbox, val, num_out, w_out, inbox_out, mw_out,
           ACT, Z, PT, PS, RSIB, RAH, RAF, RAY, RBY, RBH, RBF, RX, UPL, UP, UPT, VB, VR, VACC,
           ZS, KB, MSG, X1, WT, WR, ss, rs, credit):
    rep, fs = lax.axis_index("rep"), lax.axis_index("fsdp")
    yh, c = rep // 2, rep % 2
    z, x, yl = fs // 8, (fs // 2) % 4, fs % 2
    q = x % 2
    home = c == q
    guest = c != q
    my = 1 - yl

    def at(core, zz, xx, yy):
        return (yh * 2 + core, lax.rem(zz + 4, 4) * 8 + lax.rem(xx + 4, 4) * 2 + yy)

    sibling, mate = at(1 - c, z, x, yl), at(c, z, x, my)
    up_z, down_z = at(c, z + 1, x, yl), at(c, z + 3, x, yl)
    z0, zp, zm, z2 = z, lax.rem(z + 1, 4), lax.rem(z + 3, 4), lax.rem(z + 2, 4)
    chunk = (z2, zp, zm, z0)
    next1, next2 = (lax.rem(rep + 1, 4), fs), (lax.rem(rep + 2, 4), fs)

    names, pending = {}, {}

    def number(name):
        return names.setdefault(name, len(names))

    def remote(name, src, dst, to):
        k = number(name)
        r = number((name[0],) + name[2:]) if name[0].startswith("*") else k
        return pltpu.make_async_remote_copy(src, dst, ss.at[k], rs.at[r], device_id=to, device_id_type=MESH)

    def send(name, src, dst, to, guard=None):
        copy = remote(name, src, dst, to)
        pending[name] = (copy, guard)
        if guard is None:
            copy.start()
        else:
            pl.when(guard)(copy.start)

    def local(name, src, dst, guard):
        r = number((name[0],) + name[2:])
        pl.when(guard)(pltpu.make_async_copy(src, dst, rs.at[r]).start)

    def arrived(name, dst):
        r = number(name)
        pltpu.make_async_copy(dst, dst, rs.at[r]).wait()

    def sent(name):
        copy, guard = pending.pop(name)
        if guard is None:
            copy.wait_send()
        else:
            pl.when(guard)(copy.wait_send)

    def half(h):
        return pl.ds(pl.multiple_of(h * 128, 128), 128)

    rows_a = pl.ds(pl.multiple_of(c * 128, 64), ROUTE)
    rows_b = pl.ds(pl.multiple_of(c * 128 + ROUTE, 16), 128 - ROUTE)
    sib_a = pl.ds(pl.multiple_of((1 - c) * 128, 64), ROUTE)
    sib_b = pl.ds(pl.multiple_of((1 - c) * 128 + ROUTE, 16), 128 - ROUTE)
    hv_a, hv_b = pl.ds(0, HA), pl.ds(HA, 256 - HA)
    low, high, every = pl.ds(0, 2), pl.ds(2, 2), pl.ds(0, 4)

    def weight_at(s):
        return sc[4] if s == 0 else 0.5 * sc[4] + sc[5]

    def forward(name, s, zz, yy, mine):
        piece = Z.at[s, zz, :, yy, mine]
        send((name, s), piece, piece, sibling)

    def AX(s):
        block = num[0] if s == 0 else X1[...]
        ZS[s] = (block / weight_at(s)).astype(BF)

        def shard(h):
            return ZS.at[s, half(h)], Z.at[s, z, x, yl, half(h)]

        far = jnp.where(home, x + 2, x + 1)
        near = jnp.where(home, x, x + 3)
        send(("*AX", 0, s), *shard(0), at(0, z, far, yl))
        send(("*AX", 1, s), *shard(1), at(1, z, far, yl))
        send(("*AX", 2, s), *shard(1 - c), at(1 - c, z, near, yl))
        send(("*AX", 3, s), *shard(c), at(c, z, x + 3, yl), guest)
        local(("*AX", 4, s), *shard(c), home)

    def both_ways(plus, minus, s, piece):
        send((plus, s), piece, piece, up_z)
        send((minus, s), piece, piece, down_z)

    def AY(s):
        arrived(("*AX", s), Z.at[s, z, :, yl, half(c)])
        first, second = Z.at[s, z, :, yl, rows_a], Z.at[s, z, :, yl, rows_b]
        send(("YZy", s), first, first, mate)
        both_ways("ZYp", "ZYm", s, second)
        both_ways("YZop", "YZom", s, first)
        send(("ZYy0", s), second, second, mate)
        forward("S0", s, z, yl, half(c))

    def AY1(s):
        piece = Z.at[s, z, :, my, rows_a]
        arrived(("YZy", s), piece)
        both_ways("YZmp", "YZmm", s, piece)
        forward("S1", s, z, my, rows_a)

    def AZa(s):
        arrived(("ZYp", s), Z.at[s, zm, :, yl, rows_b])
        piece = Z.at[s, zm, low, yl, rows_b]
        send(("ZYfp", s), piece, piece, up_z)
        piece = Z.at[s, zm, :, yl, rows_b]
        send(("ZYym", s), piece, piece, mate)
        forward("Sa", s, zm, yl, rows_b)

    def AZb(s):
        arrived(("ZYm", s), Z.at[s, zp, :, yl, rows_b])
        piece = Z.at[s, zp, high, yl, rows_b]
        send(("ZYfm", s), piece, piece, down_z)
        piece = Z.at[s, zp, :, yl, rows_b]
        send(("ZYyp", s), piece, piece, mate)
        forward("Sb", s, zp, yl, rows_b)

    def AZc(s):
        arrived(("ZYfp", s), Z.at[s, z2, low, yl, rows_b])
        arrived(("ZYfm", s), Z.at[s, z2, high, yl, rows_b])
        piece = Z.at[s, z2, :, yl, rows_b]
        send(("ZYy2", s), piece, piece, mate)
        forward("Sc", s, z2, yl, rows_b)

    def AZd(s):
        piece = Z.at[s, zm, :, yl, rows_a]
        arrived(("YZop", s), piece)
        send(("YZfp", s), piece, piece, up_z)
        forward("Sd", s, zm, yl, rows_a)

    def AZe(s):
        arrived(("YZom", s), Z.at[s, zp, :, yl, rows_a])
        forward("Se", s, zp, yl, rows_a)

    def AZf(s):
        arrived(("YZmp", s), Z.at[s, zm, :, my, rows_a])
        forward("Sf", s, zm, my, rows_a)

    def AZg(s):
        piece = Z.at[s, zp, :, my, rows_a]
        arrived(("YZmm", s), piece)
        send(("YZfm", s), piece, piece, down_z)
        forward("Sg", s, zp, my, rows_a)

    def AZh(s):
        arrived(("YZfp", s), Z.at[s, z2, :, yl, rows_a])
        forward("Sh", s, z2, yl, rows_a)

    def AZi(s):
        arrived(("YZfm", s), Z.at[s, z2, :, my, rows_a])
        forward("Si", s, z2, my, rows_a)

    def AYany(source, name, zz):
        def run(s):
            arrived((source, s), Z.at[s, zz, :, my, rows_b])
            forward(name, s, zz, my, rows_b)
        return run

    def V(s, k):
        zz = chunk[k]
        if k == 3:
            arrived(("S0", s), Z.at[s, z, :, yl, half(1 - c)])
            arrived(("S1", s), Z.at[s, z, :, my, sib_a])
            arrived(("Sya", s), Z.at[s, z, :, my, sib_b])
        else:
            four = {2: ("Sa", "Sd", "Sf", "Syb"), 1: ("Sb", "Se", "Sg", "Syc"), 0: ("Sc", "Sh", "Si", "Syd")}[k]
            for name, yy, piece in zip(four, (yl, yl, my, my), (sib_b, sib_a, sib_a, sib_b)):
                arrived((name, s), Z.at[s, zz, :, yy, piece])

        def body(j, carry):
            columns = pl.ds(pl.multiple_of(zz * 2048 + j * 512, 512), 512)
            VACC[...] += jnp.dot(ACT[s, :, columns], Z[s, zz, j].reshape(512, HV), preferred_element_type=F32)
            return carry

        lax.fori_loop(0, 4, body, 0)

    def VC(s):
        VACC[...] = jnp.zeros_like(VACC)

    def VRet(s):
        VB[s] = (VACC[...] * INV_ROOT).astype(BF)
        top, low_rows = pl.ds(0, HALF_TOK), pl.ds(HALF_TOK, HALF_TOK)
        send(("*VR", 0, s), VB.at[s, top], VR.at[s, top], at(1 - c, z, x + 3, yl), guest)
        send(("*VR", 1, s), VB.at[s, low_rows], VR.at[s, low_rows], at(1 - c, z, x + 1, yl), guest)
        local(("*VR", 2, s), VB.at[s], VR.at[s], home)

    def valid(s):
        return lax.broadcasted_iota(jnp.int32, (TOK, HV), 0) < length[s]

    def VM(s):
        arrived(("*VR", s), VR.at[s])
        val[s, 0] = jnp.where(valid(s), VR[s].astype(F32), 0.0).astype(BF)

    def UPs(s):
        UPL[s] = jnp.where(valid(s), cot[s, 0].astype(F32), 0.0).astype(BF)
        top, low_rows = pl.ds(0, HALF_TOK), pl.ds(HALF_TOK, HALF_TOK)
        send(("*UP", 0, s), UPL.at[s, top], UP.at[s, top], at(1 - c, z, x + 1, yl), guest)
        send(("*UP", 1, s), UPL.at[s, low_rows], UP.at[s, low_rows], at(1 - c, z, x + 3, yl), guest)
        local(("*UP", 2, s), UPL.at[s], UP.at[s], home)

    def UT(s):
        arrived(("*UP", s), UP.at[s])
        mine = UP[s, :, pl.ds(pl.multiple_of(c * 256, 256), 256)]
        UPT[s, 0:256] = mine.astype(F32).T.astype(BF)
        other = UP[s, :, pl.ds(pl.multiple_of((1 - c) * 256, 256), 256)]
        UPT[s, 256:512] = other.astype(F32).T.astype(BF)

    def columns_of(k):
        return pl.ds(pl.multiple_of(chunk[k // 2] * 2048 + (k % 2) * SUB, SUB), SUB)

    def T(s, k):
        cols = columns_of(k)
        for j, to in ((0, x + 1), (1, x + 3)):
            rows = pl.ds(j * HALF_TOK, HALF_TOK)
            send(("*T", j, s, k), act.at[s, 0, rows, cols], ACT.at[s, rows, cols], at(1 - c, z, to, yl), guest)
        local(("*T", 2, s, k), act.at[s, 0, :, cols], ACT.at[s, :, cols], home)

    def C(s, k):
        zz = chunk[k]
        for j in (2 * k, 2 * k + 1):
            arrived(("*T", s, j), ACT.at[s, :, columns_of(j)])
        if s == 1:
            used = {0: ("Ahm", "Ahp", "Bhm", "Bhp"), 1: ("Afp", "Bfp"), 2: ("Afm", "Bfm"), 3: ("Ay",)}[k]
            for name in used:
                sent((name, 0))
            sent(("By", 0, k))
            sent(("SIB", 0, k))
            if k == 3:
                for part in range(2):
                    for j in range(4):
                        sent(("*X", j, part, 0))
            pl.semaphore_wait(credit.at[k], 1)

        def body(j, carry):
            cols = pl.ds(pl.multiple_of(zz * 2048 + j * 512, 512), 512)
            block = jnp.dot(UPT[s], ACT[s, :, cols], preferred_element_type=F32).astype(BF)
            for yy in range(2):
                PT[zz, j, yy] = block[0:256, yy * 256:(yy + 1) * 256]
                PS[zz, j, yy] = block[256:512, yy * 256:(yy + 1) * 256]
            return carry

        lax.fori_loop(0, 4, body, 0)
        send(("SIB", s, k), PS.at[zz], RSIB.at[zz], sibling)

    def add_into(count, target, *others):
        def body(j, carry):
            total = target(j)[...].astype(F32)
            for other in others:
                total = total + other(j)[...].astype(F32)
            target(j)[...] = total.astype(BF)
            return carry
        lax.fori_loop(0, count, body, 0)

    def Dd(s, k):
        zz = chunk[k]
        arrived(("SIB", s, k), RSIB.at[zz])
        add_into(8, lambda j: PT.at[zz, j // 2, j % 2], lambda j: RSIB.at[zz, j // 2, j % 2])
        if s == 0:
            pl.semaphore_signal(credit.at[k], inc=1, device_id=sibling, device_id_type=MESH)
        send(("By", s, k), PT.at[zz, :, my, hv_b], RBY.at[s, zz], mate)
        if k == 0:
            send(("Ahm", s), PT.at[zz, :, yl, hv_a], RAH.at[s, 0], down_z)
            send(("Ahp", s), PT.at[zz, :, my, hv_a], RAH.at[s, 1], up_z)

    def Ee(s, k):
        zz = chunk[k]
        arrived(("By", s, k), RBY.at[s, zz])
        add_into(4, lambda j: PT.at[zz, j, yl, hv_b], lambda j: RBY.at[s, zz, j])
        if k == 0:
            send(("Bhm", s), PT.at[zz, low, yl, hv_b], RBH.at[s, 0], down_z)
            send(("Bhp", s), PT.at[zz, high, yl, hv_b], RBH.at[s, 1], up_z)

    def Fm(s):
        arrived(("Ahm", s), RAH.at[s, 0])
        add_into(4, lambda j: PT.at[zm, j, yl, hv_a], lambda j: RAH.at[s, 0, j])
        send(("Afm", s), PT.at[zm, :, :, hv_a], RAF.at[s, 0], down_z)

    def Fp(s):
        arrived(("Ahp", s), RAH.at[s, 1])
        add_into(4, lambda j: PT.at[zp, j, my, hv_a], lambda j: RAH.at[s, 1, j])
        send(("Afp", s), PT.at[zp, :, :, hv_a], RAF.at[s, 1], up_z)

    def Gm(s):
        arrived(("Bhm", s), RBH.at[s, 0])
        add_into(2, lambda j: PT.at[zm, j, yl, hv_b], lambda j: RBH.at[s, 0, j])
        send(("Bfm", s), PT.at[zm, :, yl, hv_b], RBF.at[s, 0], down_z)

    def Gp(s):
        arrived(("Bhp", s), RBH.at[s, 1])
        add_into(2, lambda j: PT.at[zp, 2 + j, yl, hv_b], lambda j: RBH.at[s, 1, j])
        send(("Bfp", s), PT.at[zp, :, yl, hv_b], RBF.at[s, 1], up_z)

    def H(s):
        arrived(("Afm", s), RAF.at[s, 0])
        arrived(("Afp", s), RAF.at[s, 1])
        add_into(8, lambda j: PT.at[z, j // 2, j % 2, hv_a], lambda j: RAF.at[s, 0, j // 2, j % 2],
                 lambda j: RAF.at[s, 1, j // 2, j % 2])
        send(("Ay", s), PT.at[z, :, my, hv_a], RAY.at[s], mate)

    def owners(s, part, hv):
        def piece(xx, i):
            xx = lax.rem(xx, 4)
            return PT.at[z, xx, yl, hv], RX.at[s, i, c, hv]

        send(("*X", 0, part, s), *piece(x + 1, 1), at(q, z, x + 1, yl))
        send(("*X", 1, part, s), *piece(x + 3, 0), at(q, z, x + 3, yl))
        send(("*X", 2, part, s), *piece(x + 2, 1), at(q, z, x + 2, yl))
        send(("*X", 3, part, s), *piece(x, 0), sibling, guest)
        local(("*X", 4, part, s), *piece(x, 0), home)

    def I(s):
        arrived(("Ay", s), RAY.at[s])
        add_into(4, lambda j: PT.at[z, j, yl, hv_a], lambda j: RAY.at[s, j])
        owners(s, 0, hv_a)

    def J(s):
        arrived(("Bfm", s), RBF.at[s, 0])
        arrived(("Bfp", s), RBF.at[s, 1])
        add_into(4, lambda j: PT.at[z, j, yl, hv_b], lambda j: RBF.at[s, 0, j], lambda j: RBF.at[s, 1, j])
        owners(s, 1, hv_b)

    def chosen(s, which):
        return jnp.where(jnp.full((256, 256), sc[2 + s]) < 0.5, MSG[s, 0, :, which].astype(F32),
                         MSG[s, 1, :, which].astype(F32))

    def U(s):
        arrived(("*X", 0, s), RX.at[s, :, :, hv_a])
        arrived(("*X", 1, s), RX.at[s, :, :, hv_b])
        if s == 1:
            for j in range(2):
                arrived(("MSG", j, 0), MSG.at[0, j])
        for h in range(2):
            cols = slice(h * 256, (h + 1) * 256)
            grad = (RX[s, 0, h].astype(F32) + RX[s, 1, h].astype(F32)).T
            block = num[0, :, cols] if s == 0 else X1[:, cols]
            kept = 0.5 * (block - sc[s] * grad)
            KB[s, :, cols] = kept.astype(BF)
            if s == 0:
                X1[:, cols] = kept + inbox[0, :, cols]
            else:
                num_out[0, :, cols] = kept + chosen(0, cols)
        send(("MSG", 0, s), KB.at[s], MSG.at[s, 0], next1)
        send(("MSG", 1, s), KB.at[s], MSG.at[s, 1], next2)

    def M(s):
        for j in range(2):
            arrived(("WT", j), WR.at[j])
        even0, even1 = sc[2] < 0.5, sc[3] < 0.5
        w_out[0] = 0.5 * weight_at(1) + 0.5 * jnp.where(even0, WR[0, 0, 0], WR[1, 0, 0])
        mw_out[0] = 0.5 * (0.5 * jnp.where(even1, WR[0, 0, 0], WR[1, 0, 0])
                           + jnp.where(even1, WR[0, 4, 0], WR[1, 4, 0]))
        for j in range(2):
            arrived(("MSG", j, 1), MSG.at[1, j])
        for h in range(2):
            cols = slice(h * 256, (h + 1) * 256)
            inbox_out[0, :, cols] = chosen(1, cols)

    tasks = {
        "AX": AX, "AY": AY, "AY1": AY1, "AZa": AZa, "AZb": AZb, "AZc": AZc, "AZd": AZd, "AZe": AZe, "AZf": AZf,
        "AZg": AZg, "AZh": AZh, "AZi": AZi, "AYa": AYany("ZYy0", "Sya", z0), "AYb": AYany("ZYym", "Syb", zm),
        "AYc": AYany("ZYyp", "Syc", zp), "AYd": AYany("ZYy2", "Syd", z2), "V": V, "VR": VRet, "VM": VM,
        "UPs": UPs, "UT": UT, "T": T, "C": C, "D": Dd, "E": Ee, "Fm": Fm, "Fp": Fp, "Gm": Gm, "Gp": Gp,
        "H": H, "I": I, "J": J, "U": U,
    }

    barrier = pltpu.get_barrier_semaphore()
    others = [(lax.rem(rep + j, 4), fs) for j in (1, 2, 3)] + [mate, up_z, down_z]
    others += [at(core, z, x + j, yl) for core in (0, 1) for j in (1, 2, 3)]
    for other in others:
        pl.semaphore_signal(barrier, inc=1, device_id=other, device_id_type=MESH)
    pl.semaphore_wait(barrier, len(others))

    WT[...] = jnp.where(lax.broadcasted_iota(jnp.int32, (8, 128), 0) < 4, sc[4], sc[5])
    send(("WT", 0), WT, WR.at[0], next1)
    send(("WT", 1), WT, WR.at[1], next2)
    started = set()
    for entry in ORDER:
        name, *numbers = entry.split(".")
        if name == "M":
            M(0)
            continue
        if name == "V" and ("V", numbers[0]) not in started:
            started.add(("V", numbers[0]))
            VC(0)
        tasks[name](*map(int, numbers))
    for name in list(pending):
        sent(name)


def per_device(activations, cotangent, numerator, weight, inbox_num, inbox_wt, lengths, step_index):
    rate = 0.5 * math.sqrt(D / (TOK * 32)) * (1.0 + 0.5 * jnp.cos(jnp.pi * step_index.astype(F32) / 1024.0))
    scalars = jnp.concatenate([rate * INV_ROOT, (step_index % 2).astype(F32), weight, inbox_wt])
    length = lengths[:, 0, 0]
    vmem, smem, hbm = (pl.BlockSpec(memory_space=m) for m in (pltpu.VMEM, pltpu.SMEM, pl.ANY))
    hb = 256 - HA
    values, num_out, w_out, inbox_out, mw_out = pl.pallas_call(
        kernel,
        out_shape=(
            jax.ShapeDtypeStruct((2, 1, TOK, HV), BF),
            jax.ShapeDtypeStruct((1, 256, HV), F32),
            jax.ShapeDtypeStruct((1,), F32),
            jax.ShapeDtypeStruct((1, 256, HV), F32),
            jax.ShapeDtypeStruct((1,), F32),
        ),
        in_specs=[smem, smem, hbm, vmem, vmem, vmem],
        out_specs=(vmem, vmem, smem, vmem, smem),
        scratch_shapes=[
            pltpu.VMEM((2, TOK, D), BF),
            pltpu.VMEM((2, 4, 4, 2, 256, HV), BF),
            pltpu.VMEM((4, 4, 2, 256, 256), BF),
            pltpu.VMEM((4, 4, 2, 256, 256), BF),
            pltpu.VMEM((4, 4, 2, 256, 256), BF),
            pltpu.VMEM((2, 2, 4, HA, 256), BF),
            pltpu.VMEM((2, 2, 4, 2, HA, 256), BF),
            pltpu.VMEM((2, 4, HA, 256), BF),
            pltpu.VMEM((2, 4, 4, hb, 256), BF),
            pltpu.VMEM((2, 2, 2, hb, 256), BF),
            pltpu.VMEM((2, 2, 4, hb, 256), BF),
            pltpu.VMEM((2, 2, 2, 256, 256), BF),
            pltpu.VMEM((2, TOK, HV), BF),
            pltpu.VMEM((2, TOK, HV), BF),
            pltpu.VMEM((2, HV, TOK), BF),
            pltpu.VMEM((2, TOK, HV), BF),
            pltpu.VMEM((2, TOK, HV), BF),
            pltpu.VMEM((TOK, HV), F32),
            pltpu.VMEM((2, 256, HV), BF),
            pltpu.VMEM((2, 256, HV), BF),
            pltpu.VMEM((2, 2, 256, HV), BF),
            pltpu.VMEM((256, HV), F32),
            pltpu.VMEM((8, 128), F32),
            pltpu.VMEM((2, 8, 128), F32),
            pltpu.SemaphoreType.DMA((256,)),
            pltpu.SemaphoreType.DMA((256,)),
            pltpu.SemaphoreType.REGULAR((4,)),
        ],
        compiler_params=pltpu.CompilerParams(
            collective_id=0, has_side_effects=True, vmem_limit_bytes=63 * 2**20
        ),
        cost_estimate=pl.CostEstimate(flops=4 * 2 * TOK * D * HV, bytes_accessed=2 * TOK * D * 2, transcendentals=0),
        name="push_steps",
    )(scalars, length, activations, cotangent, numerator, inbox_num)
    return values, num_out, w_out, inbox_out, mw_out


def solution(mesh):
    in_specs = (
        P(None, "rep", "fsdp", None),
        P(None, "rep", "fsdp", None),
        P("rep", "fsdp", None),
        P("rep"),
        P("rep", "fsdp", None),
        P("rep"),
        P(None, "rep", "fsdp"),
        P(),
    )
    out_specs = (
        P(None, "rep", "fsdp", None),
        P("rep", "fsdp", None),
        P("rep"),
        P("rep", "fsdp", None),
        P("rep"),
    )
    return jax.shard_map(
        per_device, mesh=mesh, in_specs=in_specs, out_specs=out_specs, check_vma=False
    )
```

time: 852 us -> 172 us (0.20)
  the two profiles are of different devices: /device:TPU:18 before, /device:TPU:1 now
where the time goes in v1:
time: 172 us
  Pallas kernels  159 us (92%)
  local copies, waits for them, and re-layouts  5.8 us (3%)
  between operations  5.57 us (3%)
  other arithmetic  1.96 us (1%)
    pallas_call x1, Pallas kernels, per_device(): pl.pallas_call(kernel, out_shape=(jax.ShapeDtypeStruct((2, 1, TOK, HV), B...  159 us
    unnamed x3, local copies, waits for them, and re-layouts  5.8 us

profile of v1, /device:TPU:1, one launch (start us, length us, event | category | flops | bytes accessed | tf_op | source)
XLA Modules:
  0.0 171.9 jit_solution(14434464830188034827)
XLA Ops:
  1.9 0.7 add_multiply_fusion
  2.6 0.7 fusion
  3.3 0.6 pad_maximum_fusion.sc
  3.9 158.6 %push_steps.1 = (bf16[2,1,384,512]{3,2,1,0:T(8,128)(2,1)}, f32[1,256,512]{2,1,0:T(8,128)}, f32[1]{0:T(128)}, f32[1,256,512]{2,1,0:T(8,128)}, f32[1]{0:T(128)}) custom-call(f32[6]{0:T(128)} %pad_maximum_fusion.sc, s32[2]{0:T(128)} %bitcast.1, bf16[2,1,384,8192]{3,2,1,0:T(8,128)(2,1)} %act.1, bf16[2,1,384,512]{3,2,1,0:T(8,128)(2,1)} %cot.1, ...), custom_call_target="tpu_custom_call" | custom-call | flops 12884901888 | bytes 12582912 | tf_op jit(solution)/shard_map/push_steps/pallas_call | solution.py:430
  162.5 2.1 %copy.20 = bf16[2,1,384,512]{3,2,1,0:T(8,128)(2,1)} copy(bf16[2,1,384,512]{3,2,1,0:T(8,128)(2,1)} %get-tuple-element.10) | data formatting | bytes 1572864
  164.5 1.9 %copy.21 = f32[1,256,512]{2,1,0:T(8,128)} copy(f32[1,256,512]{2,1,0:T(8,128)} %get-tuple-element.11) | data formatting | bytes 1048576
  167.1 1.9 %copy.23 = f32[1,256,512]{2,1,0:T(8,128)} copy(f32[1,256,512]{2,1,0:T(8,128)} %get-tuple-element.13) | data formatting | bytes 1048576

commit v2 on v1

--- a/solution.py
+++ b/solution.py
@@ -13,25 +13,29 @@
 D, HV, TOK = 8192, 512, 384
 INV_ROOT = 1.0 / math.sqrt(D)
 HALF_TOK = TOK // 2
-ROUTE = 64
+ROUTE = 80
 HA = 160
 SUB = 1024
 ORDER = (
-    "UPs.0", "AX.0", "T.0.0", "T.0.1", "T.0.2", "T.0.3", "T.0.4", "T.0.5", "T.0.6", "T.0.7", "UPs.1", "UT.0",
-    "AY.0", "AZa.0", "C.0.0", "AZb.0", "AY1.0", "AYa.0", "AZe.0", "AZd.0", "D.0.0", "AZc.0", "C.0.1", "AYb.0",
-    "AZg.0", "AZf.0", "D.0.1", "AYc.0", "C.0.2", "V.0.2", "V.0.1", "E.0.0", "T.1.0", "AZh.0", "D.0.2", "Fm.0",
-    "T.1.1", "C.0.3", "AZi.0", "AYd.0", "V.0.3", "UT.1", "Fp.0", "E.0.1", "Gp.0", "T.1.2", "D.0.3", "V.0.0", "VR.0",
-    "E.0.2", "Gm.0", "T.1.3", "C.1.0", "E.0.3", "T.1.4", "VM.0", "D.1.0", "H.0", "T.1.5", "C.1.1", "E.1.0", "J.0",
-    "T.1.6", "D.1.1", "C.1.2", "I.0", "Fp.1", "T.1.7", "E.1.1", "Gp.1", "D.1.2", "Fm.1", "U.0", "AX.1", "E.1.2",
-    "Gm.1", "C.1.3", "AY.1", "D.1.3", "H.1", "AY1.1", "AZa.1", "AZb.1", "AYa.1", "AZd.1", "V.1.3", "E.1.3", "J.1",
-    "AZe.1", "AZf.1", "AZg.1", "I.1", "AZc.1", "AZh.1", "AYb.1", "U.1", "AZi.1", "V.1.2", "AYc.1", "V.1.1", "AYd.1",
+    "UPs.0", "AX.0", "T.0.0", "UT.0", "T.0.1", "AY.0", "AYz.0", "T.0.2", "AYo.0", "T.0.3", "C.0.0", "UPs.1",
+    "T.0.4", "AZa.0", "AZb.0", "AY1.0", "AYn.0", "C.0.1", "T.0.5", "T.0.6", "FS1.0", "C.0.2", "D.0.0", "AH.0",
+    "UT.1", "C.0.3", "AZc.0", "C.0.4", "FSf.0", "T.0.7", "D.0.1", "T.1.0", "AZby.0", "T.1.1", "AZd.0", "AZg.0",
+    "E.0.0", "C.0.5", "FSyd.0", "D.0.2", "FS0.0", "FSc.0", "C.0.6", "AZay.0", "FSya.0", "C.0.7", "E.0.1", "Fmm.0",
+    "Fpm.0", "T.1.2", "D.0.3", "Fpo.0", "E.0.2", "C.1.0", "Fmo.0", "T.1.3", "C.1.1", "T.1.4", "Gml.0", "Gpl.0",
+    "Hm.0", "T.1.5", "D.1.0", "Gph.0", "Gmh.0", "FSyb.0", "C.1.2", "C.1.3", "AH.1", "E.0.3", "C.1.4", "FSyc.0",
+    "FSe.0", "Ho.0", "I.0", "D.1.1", "C.1.5", "FSa.0", "Fpo.1", "J.0", "FSd.0", "E.1.0", "T.1.6", "D.1.2", "Fmm.1",
+    "Fmo.1", "U.0", "AX.1", "T.1.7", "Fpm.1", "MS.0", "C.1.6", "AY.1", "FSi.0", "FSh.0", "FSg.0", "AYn.1", "AYz.1",
+    "C.1.7", "E.1.1", "AYo.1", "FSb.0", "AZa.1", "FSa.1", "V.0.0", "D.1.3", "E.1.2", "AY1.1", "AZb.1", "V.0.2",
+    "Hm.1", "Gph.1", "AZay.1", "FSya.1", "V.0.3", "AZby.1", "Gpl.1", "V.0.1", "Gmh.1", "FS0.1", "AZd.1", "Gml.1",
+    "FSf.1", "VR.0", "AZg.1", "FS1.1", "FSe.1", "AZc.1", "Ho.1", "FSd.1", "I.1", "E.1.3", "FSyb.1", "FSg.1", "VM.0",
+    "FSc.1", "J.1", "V.1.3", "FSb.1", "V.1.2", "FSyc.1", "FSh.1", "U.1", "MS.1", "FSi.1", "FSyd.1", "V.1.1",
     "V.1.0", "VR.1", "VM.1", "M",
 )
 
 
-def kernel(sc, length, act, cot, num, inbox, val, num_out, w_out, inbox_out, mw_out,
+def kernel(index, length, weight, inbox_wt, act, cot, num, inbox, val, num_out, w_out, inbox_out, mw_out,
            ACT, Z, PT, PS, RSIB, RAH, RAF, RAY, RBY, RBH, RBF, RX, UPL, UP, UPT, VB, VR, VACC,
-           ZS, KB, MSG, X1, WT, WR, ss, rs, credit):
+           ZS, KB, MSG, X1, WT, WR, COT, NUM, INB, RATE, ss, rs, io, credit):
     rep, fs = lax.axis_index("rep"), lax.axis_index("fsdp")
     yh, c = rep // 2, rep % 2
     z, x, yl = fs // 8, (fs // 2) % 4, fs % 2
@@ -49,6 +53,10 @@
     chunk = (z2, zp, zm, z0)
     next1, next2 = (lax.rem(rep + 1, 4), fs), (lax.rem(rep + 2, 4), fs)
 
+    inputs = [pltpu.make_async_copy(*pair, io.at[i])
+              for i, pair in enumerate([(num.at[0], NUM), (cot.at[:, 0], COT), (inbox.at[0], INB)])]
+    for copy in inputs:
+        copy.start()
     names, pending = {}, {}
 
     def number(name):
@@ -93,14 +101,16 @@
     low, high, every = pl.ds(0, 2), pl.ds(2, 2), pl.ds(0, 4)
 
     def weight_at(s):
-        return sc[4] if s == 0 else 0.5 * sc[4] + sc[5]
+        return weight[0] if s == 0 else 0.5 * weight[0] + inbox_wt[0]
 
     def forward(name, s, zz, yy, mine):
         piece = Z.at[s, zz, :, yy, mine]
         send((name, s), piece, piece, sibling)
 
     def AX(s):
-        block = num[0] if s == 0 else X1[...]
+        if s == 0:
+            inputs[0].wait()
+        block = NUM[...] if s == 0 else X1[...]
         ZS[s] = (block / weight_at(s)).astype(BF)
 
         def shard(h):
@@ -118,77 +128,45 @@
         send((plus, s), piece, piece, up_z)
         send((minus, s), piece, piece, down_z)
 
+    def gathered(s, zz, yy, rows, part=every):
+        return Z.at[s, zz, part, yy, rows]
+
+    def pass_on(name, to, zz, yy, rows, source=None, part=every):
+        def run(s):
+            piece = gathered(s, zz, yy, rows, part)
+            if source is not None:
+                arrived((source, s), piece)
+            send((name, s), piece, piece, to)
+        return run
+
     def AY(s):
-        arrived(("*AX", s), Z.at[s, z, :, yl, half(c)])
-        first, second = Z.at[s, z, :, yl, rows_a], Z.at[s, z, :, yl, rows_b]
-        send(("YZy", s), first, first, mate)
-        both_ways("ZYp", "ZYm", s, second)
-        both_ways("YZop", "YZom", s, first)
-        send(("ZYy0", s), second, second, mate)
-        forward("S0", s, z, yl, half(c))
+        arrived(("*AX", s), gathered(s, z, yl, half(c)))
+        pass_on("YZy", mate, z, yl, rows_a)(s)
+
+    def AYz(s):
+        pass_on("ZYp", up_z, z, yl, rows_b)(s)
+        pass_on("ZYm", down_z, z, yl, rows_b)(s)
+
+    def AYo(s):
+        pass_on("YZop", up_z, z, yl, rows_a)(s)
+        pass_on("YZom", down_z, z, yl, rows_a)(s)
 
     def AY1(s):
-        piece = Z.at[s, z, :, my, rows_a]
-        arrived(("YZy", s), piece)
-        both_ways("YZmp", "YZmm", s, piece)
-        forward("S1", s, z, my, rows_a)
+        pass_on("YZmp", up_z, z, my, rows_a, "YZy")(s)
+        pass_on("YZmm", down_z, z, my, rows_a)(s)
 
     def AZa(s):
-        arrived(("ZYp", s), Z.at[s, zm, :, yl, rows_b])
-        piece = Z.at[s, zm, low, yl, rows_b]
-        send(("ZYfp", s), piece, piece, up_z)
-        piece = Z.at[s, zm, :, yl, rows_b]
-        send(("ZYym", s), piece, piece, mate)
-        forward("Sa", s, zm, yl, rows_b)
+        arrived(("ZYp", s), gathered(s, zm, yl, rows_b))
+        pass_on("ZYfp", up_z, zm, yl, rows_b, None, low)(s)
 
     def AZb(s):
-        arrived(("ZYm", s), Z.at[s, zp, :, yl, rows_b])
-        piece = Z.at[s, zp, high, yl, rows_b]
-        send(("ZYfm", s), piece, piece, down_z)
-        piece = Z.at[s, zp, :, yl, rows_b]
-        send(("ZYyp", s), piece, piece, mate)
-        forward("Sb", s, zp, yl, rows_b)
+        arrived(("ZYm", s), gathered(s, zp, yl, rows_b))
+        pass_on("ZYfm", down_z, zp, yl, rows_b, None, high)(s)
 
     def AZc(s):
-        arrived(("ZYfp", s), Z.at[s, z2, low, yl, rows_b])
-        arrived(("ZYfm", s), Z.at[s, z2, high, yl, rows_b])
-        piece = Z.at[s, z2, :, yl, rows_b]
-        send(("ZYy2", s), piece, piece, mate)
-        forward("Sc", s, z2, yl, rows_b)
-
-    def AZd(s):
-        piece = Z.at[s, zm, :, yl, rows_a]
-        arrived(("YZop", s), piece)
-        send(("YZfp", s), piece, piece, up_z)
-        forward("Sd", s, zm, yl, rows_a)
-
-    def AZe(s):
-        arrived(("YZom", s), Z.at[s, zp, :, yl, rows_a])
-        forward("Se", s, zp, yl, rows_a)
-
-    def AZf(s):
-        arrived(("YZmp", s), Z.at[s, zm, :, my, rows_a])
-        forward("Sf", s, zm, my, rows_a)
-
-    def AZg(s):
-        piece = Z.at[s, zp, :, my, rows_a]
-        arrived(("YZmm", s), piece)
-        send(("YZfm", s), piece, piece, down_z)
-        forward("Sg", s, zp, my, rows_a)
-
-    def AZh(s):
-        arrived(("YZfp", s), Z.at[s, z2, :, yl, rows_a])
-        forward("Sh", s, z2, yl, rows_a)
-
-    def AZi(s):
-        arrived(("YZfm", s), Z.at[s, z2, :, my, rows_a])
-        forward("Si", s, z2, my, rows_a)
-
-    def AYany(source, name, zz):
-        def run(s):
-            arrived((source, s), Z.at[s, zz, :, my, rows_b])
-            forward(name, s, zz, my, rows_b)
-        return run
+        arrived(("ZYfp", s), gathered(s, z2, yl, rows_b, low))
+        arrived(("ZYfm", s), gathered(s, z2, yl, rows_b, high))
+        pass_on("ZYy2", mate, z2, yl, rows_b)(s)
 
     def V(s, k):
         zz = chunk[k]
@@ -223,10 +201,19 @@
 
     def VM(s):
         arrived(("*VR", s), VR.at[s])
-        val[s, 0] = jnp.where(valid(s), VR[s].astype(F32), 0.0).astype(BF)
+        VR[s] = jnp.where(valid(s), VR[s].astype(F32), 0.0).astype(BF)
+        result(VR.at[s], val.at[s, 0])
+
+    outputs = []
+
+    def result(src, dst):
+        outputs.append(pltpu.make_async_copy(src, dst, io.at[3 + len(outputs)]))
+        outputs[-1].start()
 
     def UPs(s):
-        UPL[s] = jnp.where(valid(s), cot[s, 0].astype(F32), 0.0).astype(BF)
+        if s == 0:
+            inputs[1].wait()
+        UPL[s] = jnp.where(valid(s), COT[s].astype(F32), 0.0).astype(BF)
         top, low_rows = pl.ds(0, HALF_TOK), pl.ds(HALF_TOK, HALF_TOK)
         send(("*UP", 0, s), UPL.at[s, top], UP.at[s, top], at(1 - c, z, x + 1, yl), guest)
         send(("*UP", 1, s), UPL.at[s, low_rows], UP.at[s, low_rows], at(1 - c, z, x + 3, yl), guest)
@@ -250,20 +237,21 @@
         local(("*T", 2, s, k), act.at[s, 0, :, cols], ACT.at[s, :, cols], home)
 
     def C(s, k):
-        zz = chunk[k]
-        for j in (2 * k, 2 * k + 1):
-            arrived(("*T", s, j), ACT.at[s, :, columns_of(j)])
-        if s == 1:
-            used = {0: ("Ahm", "Ahp", "Bhm", "Bhp"), 1: ("Afp", "Bfp"), 2: ("Afm", "Bfm"), 3: ("Ay",)}[k]
+        zz = chunk[k // 2]
+        arrived(("*T", s, k), ACT.at[s, :, columns_of(k)])
+        if s == 1 and k % 2 == 0:
+            used = {0: ("Ahm", "Ahp", "Bhm", "Bhp"), 1: ("Afpo", "Afpm", "Bfpl", "Bfph"),
+                    2: ("Afmo", "Afmm", "Bfml", "Bfmh"), 3: ("Ay",)}[k // 2]
             for name in used:
                 sent((name, 0))
-            sent(("By", 0, k))
+            sent(("By", 0, k // 2))
             sent(("SIB", 0, k))
-            if k == 3:
+            sent(("SIB", 0, k + 1))
+            if k == 6:
                 for part in range(2):
                     for j in range(4):
                         sent(("*X", j, part, 0))
-            pl.semaphore_wait(credit.at[k], 1)
+            pl.semaphore_wait(credit.at[k // 2], 1)
 
         def body(j, carry):
             cols = pl.ds(pl.multiple_of(zz * 2048 + j * 512, 512), 512)
@@ -273,8 +261,10 @@
                 PS[zz, j, yy] = block[256:512, yy * 256:(yy + 1) * 256]
             return carry
 
-        lax.fori_loop(0, 4, body, 0)
-        send(("SIB", s, k), PS.at[zz], RSIB.at[zz], sibling)
+        first = 2 * (k % 2)
+        lax.fori_loop(first, first + 2, body, 0)
+        pair = pl.ds(first, 2)
+        send(("SIB", s, k), PS.at[zz, pair], RSIB.at[zz, pair], sibling)
 
     def add_into(count, target, *others):
         def body(j, carry):
@@ -287,14 +277,16 @@
 
     def Dd(s, k):
         zz = chunk[k]
-        arrived(("SIB", s, k), RSIB.at[zz])
+        arrived(("SIB", s, 2 * k), RSIB.at[zz, low])
+        arrived(("SIB", s, 2 * k + 1), RSIB.at[zz, high])
         add_into(8, lambda j: PT.at[zz, j // 2, j % 2], lambda j: RSIB.at[zz, j // 2, j % 2])
         if s == 0:
             pl.semaphore_signal(credit.at[k], inc=1, device_id=sibling, device_id_type=MESH)
         send(("By", s, k), PT.at[zz, :, my, hv_b], RBY.at[s, zz], mate)
-        if k == 0:
-            send(("Ahm", s), PT.at[zz, :, yl, hv_a], RAH.at[s, 0], down_z)
-            send(("Ahp", s), PT.at[zz, :, my, hv_a], RAH.at[s, 1], up_z)
+
+    def AH(s):
+        send(("Ahm", s), PT.at[z2, :, yl, hv_a], RAH.at[s, 0], down_z)
+        send(("Ahp", s), PT.at[z2, :, my, hv_a], RAH.at[s, 1], up_z)
 
     def Ee(s, k):
         zz = chunk[k]
@@ -304,32 +296,49 @@
             send(("Bhm", s), PT.at[zz, low, yl, hv_b], RBH.at[s, 0], down_z)
             send(("Bhp", s), PT.at[zz, high, yl, hv_b], RBH.at[s, 1], up_z)
 
-    def Fm(s):
+    def Fmm(s):
+        send(("Afmm", s), PT.at[zm, :, my, hv_a], RAF.at[s, 0, :, my], down_z)
+
+    def Fmo(s):
         arrived(("Ahm", s), RAH.at[s, 0])
         add_into(4, lambda j: PT.at[zm, j, yl, hv_a], lambda j: RAH.at[s, 0, j])
-        send(("Afm", s), PT.at[zm, :, :, hv_a], RAF.at[s, 0], down_z)
-
-    def Fp(s):
+        send(("Afmo", s), PT.at[zm, :, yl, hv_a], RAF.at[s, 0, :, yl], down_z)
+
+    def Fpo(s):
+        send(("Afpo", s), PT.at[zp, :, yl, hv_a], RAF.at[s, 1, :, yl], up_z)
+
+    def Fpm(s):
         arrived(("Ahp", s), RAH.at[s, 1])
         add_into(4, lambda j: PT.at[zp, j, my, hv_a], lambda j: RAH.at[s, 1, j])
-        send(("Afp", s), PT.at[zp, :, :, hv_a], RAF.at[s, 1], up_z)
-
-    def Gm(s):
+        send(("Afpm", s), PT.at[zp, :, my, hv_a], RAF.at[s, 1, :, my], up_z)
+
+    def Gmh(s):
+        send(("Bfmh", s), PT.at[zm, high, yl, hv_b], RBF.at[s, 0, high], down_z)
+
+    def Gml(s):
         arrived(("Bhm", s), RBH.at[s, 0])
         add_into(2, lambda j: PT.at[zm, j, yl, hv_b], lambda j: RBH.at[s, 0, j])
-        send(("Bfm", s), PT.at[zm, :, yl, hv_b], RBF.at[s, 0], down_z)
-
-    def Gp(s):
+        send(("Bfml", s), PT.at[zm, low, yl, hv_b], RBF.at[s, 0, low], down_z)
+
+    def Gpl(s):
+        send(("Bfpl", s), PT.at[zp, low, yl, hv_b], RBF.at[s, 1, low], up_z)
+
+    def Gph(s):
         arrived(("Bhp", s), RBH.at[s, 1])
         add_into(2, lambda j: PT.at[zp, 2 + j, yl, hv_b], lambda j: RBH.at[s, 1, j])
-        send(("Bfp", s), PT.at[zp, :, yl, hv_b], RBF.at[s, 1], up_z)
-
-    def H(s):
-        arrived(("Afm", s), RAF.at[s, 0])
-        arrived(("Afp", s), RAF.at[s, 1])
-        add_into(8, lambda j: PT.at[z, j // 2, j % 2, hv_a], lambda j: RAF.at[s, 0, j // 2, j % 2],
-                 lambda j: RAF.at[s, 1, j // 2, j % 2])
+        send(("Bfph", s), PT.at[zp, high, yl, hv_b], RBF.at[s, 1, high], up_z)
+
+    def H(s, yy, minus, plus):
+        arrived((minus, s), RAF.at[s, 0, :, yy])
+        arrived((plus, s), RAF.at[s, 1, :, yy])
+        add_into(4, lambda j: PT.at[z, j, yy, hv_a], lambda j: RAF.at[s, 0, j, yy], lambda j: RAF.at[s, 1, j, yy])
+
+    def Hm(s):
+        H(s, my, "Afmm", "Afpm")
         send(("Ay", s), PT.at[z, :, my, hv_a], RAY.at[s], mate)
+
+    def Ho(s):
+        H(s, yl, "Afmo", "Afpo")
 
     def owners(s, part, hv):
         def piece(xx, i):
@@ -348,38 +357,47 @@
         owners(s, 0, hv_a)
 
     def J(s):
-        arrived(("Bfm", s), RBF.at[s, 0])
-        arrived(("Bfp", s), RBF.at[s, 1])
+        for name, way, part in (("Bfml", 0, low), ("Bfmh", 0, high), ("Bfpl", 1, low), ("Bfph", 1, high)):
+            arrived((name, s), RBF.at[s, way, part])
         add_into(4, lambda j: PT.at[z, j, yl, hv_b], lambda j: RBF.at[s, 0, j], lambda j: RBF.at[s, 1, j])
         owners(s, 1, hv_b)
 
     def chosen(s, which):
-        return jnp.where(jnp.full((256, 256), sc[2 + s]) < 0.5, MSG[s, 0, :, which].astype(F32),
+        return jnp.where(jnp.full((256, 256), index[s] % 2) == 0, MSG[s, 0, :, which].astype(F32),
                          MSG[s, 1, :, which].astype(F32))
 
     def U(s):
         arrived(("*X", 0, s), RX.at[s, :, :, hv_a])
         arrived(("*X", 1, s), RX.at[s, :, :, hv_b])
+        if s == 0:
+            inputs[2].wait()
+            for j in range(2):
+                step = jnp.full((8, 128), index[j]).astype(F32)
+                RATE[j] = 0.5 * math.sqrt(D / (TOK * 32)) * INV_ROOT * (1.0 + 0.5 * jnp.cos(jnp.pi * step / 1024.0))
         if s == 1:
             for j in range(2):
                 arrived(("MSG", j, 0), MSG.at[0, j])
         for h in range(2):
             cols = slice(h * 256, (h + 1) * 256)
             grad = (RX[s, 0, h].astype(F32) + RX[s, 1, h].astype(F32)).T
-            block = num[0, :, cols] if s == 0 else X1[:, cols]
-            kept = 0.5 * (block - sc[s] * grad)
+            block = NUM[:, cols] if s == 0 else X1[:, cols]
+            kept = 0.5 * (block - RATE[s, 0:1, 0:1] * grad)
             KB[s, :, cols] = kept.astype(BF)
             if s == 0:
-                X1[:, cols] = kept + inbox[0, :, cols]
+                X1[:, cols] = kept + INB[:, cols]
             else:
-                num_out[0, :, cols] = kept + chosen(0, cols)
+                X1[:, cols] = kept + chosen(0, cols)
+        if s == 1:
+            result(X1, num_out.at[0])
+
+    def MS(s):
         send(("MSG", 0, s), KB.at[s], MSG.at[s, 0], next1)
         send(("MSG", 1, s), KB.at[s], MSG.at[s, 1], next2)
 
     def M(s):
         for j in range(2):
             arrived(("WT", j), WR.at[j])
-        even0, even1 = sc[2] < 0.5, sc[3] < 0.5
+        even0, even1 = index[0] % 2 == 0, index[1] % 2 == 0
         w_out[0] = 0.5 * weight_at(1) + 0.5 * jnp.where(even0, WR[0, 0, 0], WR[1, 0, 0])
         mw_out[0] = 0.5 * (0.5 * jnp.where(even1, WR[0, 0, 0], WR[1, 0, 0])
                            + jnp.where(even1, WR[0, 4, 0], WR[1, 4, 0]))
@@ -387,14 +405,25 @@
             arrived(("MSG", j, 1), MSG.at[1, j])
         for h in range(2):
             cols = slice(h * 256, (h + 1) * 256)
-            inbox_out[0, :, cols] = chosen(1, cols)
+            INB[:, cols] = chosen(1, cols)
+        result(INB, inbox_out.at[0])
 
     tasks = {
-        "AX": AX, "AY": AY, "AY1": AY1, "AZa": AZa, "AZb": AZb, "AZc": AZc, "AZd": AZd, "AZe": AZe, "AZf": AZf,
-        "AZg": AZg, "AZh": AZh, "AZi": AZi, "AYa": AYany("ZYy0", "Sya", z0), "AYb": AYany("ZYym", "Syb", zm),
-        "AYc": AYany("ZYyp", "Syc", zp), "AYd": AYany("ZYy2", "Syd", z2), "V": V, "VR": VRet, "VM": VM,
-        "UPs": UPs, "UT": UT, "T": T, "C": C, "D": Dd, "E": Ee, "Fm": Fm, "Fp": Fp, "Gm": Gm, "Gp": Gp,
-        "H": H, "I": I, "J": J, "U": U,
+        "AX": AX, "AY": AY, "AYz": AYz, "AYo": AYo, "AYn": pass_on("ZYy0", mate, z, yl, rows_b), "AY1": AY1,
+        "AZa": AZa, "AZb": AZb, "AZc": AZc,
+        "AZay": pass_on("ZYym", mate, zm, yl, rows_b), "AZby": pass_on("ZYyp", mate, zp, yl, rows_b),
+        "AZd": pass_on("YZfp", up_z, zm, yl, rows_a, "YZop"), "AZg": pass_on("YZfm", down_z, zp, my, rows_a, "YZmm"),
+        "FS0": pass_on("S0", sibling, z, yl, half(c)), "FS1": pass_on("S1", sibling, z, my, rows_a),
+        "FSa": pass_on("Sa", sibling, zm, yl, rows_b), "FSb": pass_on("Sb", sibling, zp, yl, rows_b),
+        "FSc": pass_on("Sc", sibling, z2, yl, rows_b), "FSd": pass_on("Sd", sibling, zm, yl, rows_a),
+        "FSe": pass_on("Se", sibling, zp, yl, rows_a, "YZom"), "FSf": pass_on("Sf", sibling, zm, my, rows_a, "YZmp"),
+        "FSg": pass_on("Sg", sibling, zp, my, rows_a), "FSh": pass_on("Sh", sibling, z2, yl, rows_a, "YZfp"),
+        "FSi": pass_on("Si", sibling, z2, my, rows_a, "YZfm"),
+        "FSya": pass_on("Sya", sibling, z0, my, rows_b, "ZYy0"), "FSyb": pass_on("Syb", sibling, zm, my, rows_b, "ZYym"),
+        "FSyc": pass_on("Syc", sibling, zp, my, rows_b, "ZYyp"), "FSyd": pass_on("Syd", sibling, z2, my, rows_b, "ZYy2"),
+        "V": V, "VR": VRet, "VM": VM, "UPs": UPs, "UT": UT, "T": T, "C": C, "D": Dd, "E": Ee, "AH": AH,
+        "Fmm": Fmm, "Fmo": Fmo, "Fpo": Fpo, "Fpm": Fpm, "Gmh": Gmh, "Gml": Gml, "Gpl": Gpl, "Gph": Gph,
+        "Hm": Hm, "Ho": Ho, "I": I, "J": J, "U": U, "MS": MS,
     }
 
     barrier = pltpu.get_barrier_semaphore()
@@ -404,7 +433,7 @@
         pl.semaphore_signal(barrier, inc=1, device_id=other, device_id_type=MESH)
     pl.semaphore_wait(barrier, len(others))
 
-    WT[...] = jnp.where(lax.broadcasted_iota(jnp.int32, (8, 128), 0) < 4, sc[4], sc[5])
+    WT[...] = jnp.where(lax.broadcasted_iota(jnp.int32, (8, 128), 0) < 4, weight[0], inbox_wt[0])
     send(("WT", 0), WT, WR.at[0], next1)
     send(("WT", 1), WT, WR.at[1], next2)
     started = set()
@@ -419,25 +448,36 @@
         tasks[name](*map(int, numbers))
     for name in list(pending):
         sent(name)
+    for copy in outputs:
+        copy.wait()
+
+
+def finish(val, num_out, inbox_out, w_out, mw_out, val_to, num_to, inbox_to, w_to, mw_to, VAL, NUM, INB, sem):
+    trips = [(val, VAL, val_to), (num_out, NUM, num_to), (inbox_out, INB, inbox_to)]
+    loads = [pltpu.make_async_copy(src, stop, sem.at[i]) for i, (src, stop, dst) in enumerate(trips)]
+    stores = [pltpu.make_async_copy(stop, dst, sem.at[3 + i]) for i, (src, stop, dst) in enumerate(trips)]
+    for copy in loads:
+        copy.start()
+    w_to[0] = w_out[0]
+    mw_to[0] = mw_out[0]
+    for load, store in zip(loads, stores):
+        load.wait()
+        store.start()
+    for copy in stores:
+        copy.wait()
 
 
 def per_device(activations, cotangent, numerator, weight, inbox_num, inbox_wt, lengths, step_index):
-    rate = 0.5 * math.sqrt(D / (TOK * 32)) * (1.0 + 0.5 * jnp.cos(jnp.pi * step_index.astype(F32) / 1024.0))
-    scalars = jnp.concatenate([rate * INV_ROOT, (step_index % 2).astype(F32), weight, inbox_wt])
-    length = lengths[:, 0, 0]
-    vmem, smem, hbm = (pl.BlockSpec(memory_space=m) for m in (pltpu.VMEM, pltpu.SMEM, pl.ANY))
+    smem, hbm = (pl.BlockSpec(memory_space=m) for m in (pltpu.SMEM, pl.ANY))
     hb = 256 - HA
+    matrix = jax.ShapeDtypeStruct((1, 256, HV), F32)
+    scalar = jax.ShapeDtypeStruct((1,), F32)
+    tokens = jax.ShapeDtypeStruct((2, 1, TOK, HV), BF)
     values, num_out, w_out, inbox_out, mw_out = pl.pallas_call(
         kernel,
-        out_shape=(
-            jax.ShapeDtypeStruct((2, 1, TOK, HV), BF),
-            jax.ShapeDtypeStruct((1, 256, HV), F32),
-            jax.ShapeDtypeStruct((1,), F32),
-            jax.ShapeDtypeStruct((1, 256, HV), F32),
-            jax.ShapeDtypeStruct((1,), F32),
-        ),
-        in_specs=[smem, smem, hbm, vmem, vmem, vmem],
-        out_specs=(vmem, vmem, smem, vmem, smem),
+        out_shape=(tokens, matrix, scalar, matrix, scalar),
+        in_specs=[smem] * 4 + [hbm] * 4,
+        out_specs=(hbm, hbm, smem, hbm, smem),
         scratch_shapes=[
             pltpu.VMEM((2, TOK, D), BF),
             pltpu.VMEM((2, 4, 4, 2, 256, HV), BF),
@@ -463,8 +503,13 @@
             pltpu.VMEM((256, HV), F32),
             pltpu.VMEM((8, 128), F32),
             pltpu.VMEM((2, 8, 128), F32),
+            pltpu.VMEM((2, TOK, HV), BF),
+            pltpu.VMEM((256, HV), F32),
+            pltpu.VMEM((256, HV), F32),
+            pltpu.VMEM((2, 8, 128), F32),
             pltpu.SemaphoreType.DMA((256,)),
             pltpu.SemaphoreType.DMA((256,)),
+            pltpu.SemaphoreType.DMA((8,)),
             pltpu.SemaphoreType.REGULAR((4,)),
         ],
         compiler_params=pltpu.CompilerParams(
@@ -472,7 +517,20 @@
         ),
         cost_estimate=pl.CostEstimate(flops=4 * 2 * TOK * D * HV, bytes_accessed=2 * TOK * D * 2, transcendentals=0),
         name="push_steps",
-    )(scalars, length, activations, cotangent, numerator, inbox_num)
+    )(step_index, lengths[:, 0, 0], weight, inbox_wt, activations, cotangent, numerator, inbox_num)
+    values, num_out, inbox_out, w_out, mw_out = pl.pallas_call(
+        finish,
+        out_shape=(tokens, matrix, matrix, scalar, scalar),
+        in_specs=[hbm] * 3 + [smem] * 2,
+        out_specs=(hbm,) * 3 + (smem,) * 2,
+        scratch_shapes=[
+            pltpu.VMEM((2, 1, TOK, HV), BF),
+            pltpu.VMEM((1, 256, HV), F32),
+            pltpu.VMEM((1, 256, HV), F32),
+            pltpu.SemaphoreType.DMA((6,)),
+        ],
+        name="finish",
+    )(values, num_out, inbox_out, w_out, mw_out)
     return values, num_out, w_out, inbox_out, mw_out
 
 

time: 172 us -> 157 us (0.913)
  local copies, waits for them, and re-layouts: 5.8 us -> 0 us
  Pallas kernels: 159 us -> 154 us
  between operations: 5.57 us -> 1.93 us
  other arithmetic: 1.96 us -> 0 us
    unnamed x3 -> x0, local copies, waits for them, and re-layouts: 5.8 us -> none
    pallas_call x1 -> x2, Pallas kernels: 159 us -> 154 us  [the longest x1 150 us: per_device(): pl.pallas_call(kernel, out_shape=(tokens, matrix, scalar, matrix, scalar)...]
where the time goes in v2:
time: 157 us; the launch traced here: 156 us
  Pallas kernels  154 us (98%)
  between operations  1.93 us (1%)
    pallas_call x1, Pallas kernels, per_device(): pl.pallas_call(kernel, out_shape=(tokens, matrix, scalar, matrix, scalar)...  150 us
    pallas_call x1, Pallas kernels, per_device(): pl.pallas_call(finish, out_shape=(tokens, matrix, matrix, scalar, scalar)...  4.24 us

profile of v2, /device:TPU:1, one launch (start us, length us, event | category | flops | bytes accessed | tf_op | source)
XLA Modules:
  0.0 156.4 jit_solution(2350113310174944640)
XLA Ops:
  1.9 150.2 %push_steps.1 = (bf16[2,1,384,512]{3,2,1,0:T(8,128)(2,1)}, f32[1,256,512]{2,1,0:T(8,128)}, f32[1]{0:T(128)}, f32[1,256,512]{2,1,0:T(8,128)}, f32[1]{0:T(128)}) custom-call(s32[2]{0:T(128)} %index.1, s32[2]{0:T(128)} %bitcast.1, f32[1]{0:T(128)S(6)} %copy.13.weight, f32[1]{0:T(128)S(6)} %copy.14.inbox_wt, bf16[2,1,384,8192]{3,2,1,0:T(8,128)(2,1)} %act.1, ...), custom_call_target="tpu_custom_call" | custom-call | flops 12884901888 | bytes 12582912 | tf_op jit(solution)/shard_map/push_steps/pallas_call | solution.py:476
  152.1 4.2 %finish.1 = (bf16[2,1,384,512]{3,2,1,0:T(8,128)(2,1)}, f32[1,256,512]{2,1,0:T(8,128)}, f32[1,256,512]{2,1,0:T(8,128)}, f32[1]{0:T(128)}, f32[1]{0:T(128)}) custom-call(bf16[2,1,384,512]{3,2,1,0:T(8,128)(2,1)} %get-tuple-element.15.val, f32[1,256,512]{2,1,0:T(8,128)} %get-tuple-element.16.num_out, f32[1,256,512]{2,1,0:T(8,128)} %get-tuple-element.17.inbox_out, ...), custom_call_target="tpu_custom_call" | custom-call | tf_op jit(solution)/shard_map/finish/pallas_call | solution.py:521

commit v3 on v2

--- a/solution.py
+++ b/solution.py
@@ -13,24 +13,9 @@
 D, HV, TOK = 8192, 512, 384
 INV_ROOT = 1.0 / math.sqrt(D)
 HALF_TOK = TOK // 2
-ROUTE = 80
-HA = 160
+ROUTE = 96
+HA = 128
 SUB = 1024
-ORDER = (
-    "UPs.0", "AX.0", "T.0.0", "UT.0", "T.0.1", "AY.0", "AYz.0", "T.0.2", "AYo.0", "T.0.3", "C.0.0", "UPs.1",
-    "T.0.4", "AZa.0", "AZb.0", "AY1.0", "AYn.0", "C.0.1", "T.0.5", "T.0.6", "FS1.0", "C.0.2", "D.0.0", "AH.0",
-    "UT.1", "C.0.3", "AZc.0", "C.0.4", "FSf.0", "T.0.7", "D.0.1", "T.1.0", "AZby.0", "T.1.1", "AZd.0", "AZg.0",
-    "E.0.0", "C.0.5", "FSyd.0", "D.0.2", "FS0.0", "FSc.0", "C.0.6", "AZay.0", "FSya.0", "C.0.7", "E.0.1", "Fmm.0",
-    "Fpm.0", "T.1.2", "D.0.3", "Fpo.0", "E.0.2", "C.1.0", "Fmo.0", "T.1.3", "C.1.1", "T.1.4", "Gml.0", "Gpl.0",
-    "Hm.0", "T.1.5", "D.1.0", "Gph.0", "Gmh.0", "FSyb.0", "C.1.2", "C.1.3", "AH.1", "E.0.3", "C.1.4", "FSyc.0",
-    "FSe.0", "Ho.0", "I.0", "D.1.1", "C.1.5", "FSa.0", "Fpo.1", "J.0", "FSd.0", "E.1.0", "T.1.6", "D.1.2", "Fmm.1",
-    "Fmo.1", "U.0", "AX.1", "T.1.7", "Fpm.1", "MS.0", "C.1.6", "AY.1", "FSi.0", "FSh.0", "FSg.0", "AYn.1", "AYz.1",
-    "C.1.7", "E.1.1", "AYo.1", "FSb.0", "AZa.1", "FSa.1", "V.0.0", "D.1.3", "E.1.2", "AY1.1", "AZb.1", "V.0.2",
-    "Hm.1", "Gph.1", "AZay.1", "FSya.1", "V.0.3", "AZby.1", "Gpl.1", "V.0.1", "Gmh.1", "FS0.1", "AZd.1", "Gml.1",
-    "FSf.1", "VR.0", "AZg.1", "FS1.1", "FSe.1", "AZc.1", "Ho.1", "FSd.1", "I.1", "E.1.3", "FSyb.1", "FSg.1", "VM.0",
-    "FSc.1", "J.1", "V.1.3", "FSb.1", "V.1.2", "FSyc.1", "FSh.1", "U.1", "MS.1", "FSi.1", "FSyd.1", "V.1.1",
-    "V.1.0", "VR.1", "VM.1", "M",
-)
 
 
 def kernel(index, length, weight, inbox_wt, act, cot, num, inbox, val, num_out, w_out, inbox_out, mw_out,
@@ -99,34 +84,29 @@
     sib_b = pl.ds(pl.multiple_of((1 - c) * 128 + ROUTE, 16), 128 - ROUTE)
     hv_a, hv_b = pl.ds(0, HA), pl.ds(HA, 256 - HA)
     low, high, every = pl.ds(0, 2), pl.ds(2, 2), pl.ds(0, 4)
+    own, rest = pl.ds(0, 1), pl.ds(1, 3)
 
     def weight_at(s):
         return weight[0] if s == 0 else 0.5 * weight[0] + inbox_wt[0]
 
-    def forward(name, s, zz, yy, mine):
-        piece = Z.at[s, zz, :, yy, mine]
-        send((name, s), piece, piece, sibling)
-
-    def AX(s):
-        if s == 0:
-            inputs[0].wait()
+    def project(s):
         block = NUM[...] if s == 0 else X1[...]
         ZS[s] = (block / weight_at(s)).astype(BF)
 
-        def shard(h):
-            return ZS.at[s, half(h)], Z.at[s, z, x, yl, half(h)]
-
-        far = jnp.where(home, x + 2, x + 1)
-        near = jnp.where(home, x, x + 3)
-        send(("*AX", 0, s), *shard(0), at(0, z, far, yl))
-        send(("*AX", 1, s), *shard(1), at(1, z, far, yl))
-        send(("*AX", 2, s), *shard(1 - c), at(1 - c, z, near, yl))
-        send(("*AX", 3, s), *shard(c), at(c, z, x + 3, yl), guest)
-        local(("*AX", 4, s), *shard(c), home)
-
-    def both_ways(plus, minus, s, piece):
-        send((plus, s), piece, piece, up_z)
-        send((minus, s), piece, piece, down_z)
+    def AX(s):
+        if s == 1:
+            project(s)
+
+        def shard(h, place):
+            return ZS.at[s, half(h)], Z.at[s, z, place, yl, half(h)]
+
+        send(("*AXo", 0, s), *shard(1 - c, 0), sibling, home)
+        local(("*AXo", 1, s), *shard(c, 0), home)
+        far, place = jnp.where(home, x + 2, x + 1), jnp.where(home, 2, 3)
+        send(("*AX", 0, s), *shard(0, place), at(0, z, far, yl))
+        send(("*AX", 1, s), *shard(1, place), at(1, z, far, yl))
+        send(("*AX", 2, s), *shard(0, 1), at(0, z, x + 3, yl), guest)
+        send(("*AX", 3, s), *shard(1, 1), at(1, z, x + 3, yl), guest)
 
     def gathered(s, zz, yy, rows, part=every):
         return Z.at[s, zz, part, yy, rows]
@@ -134,33 +114,52 @@
     def pass_on(name, to, zz, yy, rows, source=None, part=every):
         def run(s):
             piece = gathered(s, zz, yy, rows, part)
-            if source is not None:
+            if source in ("YZop", "YZom", "YZmp", "YZmm", "ZYy0"):
+                both(source, s, zz, yy, rows)
+            elif source is not None:
                 arrived((source, s), piece)
             send((name, s), piece, piece, to)
         return run
 
-    def AY(s):
-        arrived(("*AX", s), gathered(s, z, yl, half(c)))
-        pass_on("YZy", mate, z, yl, rows_a)(s)
-
-    def AYz(s):
-        pass_on("ZYp", up_z, z, yl, rows_b)(s)
-        pass_on("ZYm", down_z, z, yl, rows_b)(s)
-
-    def AYo(s):
-        pass_on("YZop", up_z, z, yl, rows_a)(s)
-        pass_on("YZom", down_z, z, yl, rows_a)(s)
+    def both(name, s, zz, yy, rows):
+        arrived((name, 0, s), gathered(s, zz, yy, rows, own))
+        arrived((name, 1, s), gathered(s, zz, yy, rows, rest))
+
+    def first_hop(plus, minus, rows, part, yy=yl):
+        def run(s):
+            piece = gathered(s, z, yy, rows, part)
+            send((plus, int(part is rest), s), piece, piece, up_z)
+            send((minus, int(part is rest), s), piece, piece, down_z)
+        return run
+
+    def to_mate(name, rows, part):
+        def run(s):
+            piece = gathered(s, z, yl, rows, part)
+            send((name, int(part is rest), s), piece, piece, mate)
+        return run
+
+    def AYp(s):
+        arrived(("*AXo", s), gathered(s, z, yl, half(c), own))
+        to_mate("YZy", rows_a, own)(s)
+
+    def AYq(s):
+        arrived(("*AX", s), gathered(s, z, yl, half(c), rest))
+        to_mate("YZy", rows_a, rest)(s)
+
+    def AY1p(s):
+        arrived(("YZy", 0, s), gathered(s, z, my, rows_a, own))
+        first_hop("YZmp", "YZmm", rows_a, own, my)(s)
 
     def AY1(s):
-        pass_on("YZmp", up_z, z, my, rows_a, "YZy")(s)
-        pass_on("YZmm", down_z, z, my, rows_a)(s)
+        arrived(("YZy", 1, s), gathered(s, z, my, rows_a, rest))
+        first_hop("YZmp", "YZmm", rows_a, rest, my)(s)
 
     def AZa(s):
-        arrived(("ZYp", s), gathered(s, zm, yl, rows_b))
+        both("ZYp", s, zm, yl, rows_b)
         pass_on("ZYfp", up_z, zm, yl, rows_b, None, low)(s)
 
     def AZb(s):
-        arrived(("ZYm", s), gathered(s, zp, yl, rows_b))
+        both("ZYm", s, zp, yl, rows_b)
         pass_on("ZYfm", down_z, zp, yl, rows_b, None, high)(s)
 
     def AZc(s):
@@ -168,8 +167,13 @@
         arrived(("ZYfm", s), gathered(s, z2, yl, rows_b, high))
         pass_on("ZYy2", mate, z2, yl, rows_b)(s)
 
+    begun = set()
+
     def V(s, k):
         zz = chunk[k]
+        if s not in begun:
+            begun.add(s)
+            VACC[...] = jnp.zeros_like(VACC)
         if k == 3:
             arrived(("S0", s), Z.at[s, z, :, yl, half(1 - c)])
             arrived(("S1", s), Z.at[s, z, :, my, sib_a])
@@ -180,14 +184,11 @@
                 arrived((name, s), Z.at[s, zz, :, yy, piece])
 
         def body(j, carry):
-            columns = pl.ds(pl.multiple_of(zz * 2048 + j * 512, 512), 512)
+            columns = pl.ds(pl.multiple_of(zz * 2048 + lax.rem(x + j, 4) * 512, 512), 512)
             VACC[...] += jnp.dot(ACT[s, :, columns], Z[s, zz, j].reshape(512, HV), preferred_element_type=F32)
             return carry
 
         lax.fori_loop(0, 4, body, 0)
-
-    def VC(s):
-        VACC[...] = jnp.zeros_like(VACC)
 
     def VRet(s):
         VB[s] = (VACC[...] * INV_ROOT).astype(BF)
@@ -211,9 +212,6 @@
         outputs[-1].start()
 
     def UPs(s):
-        if s == 0:
-            inputs[1].wait()
-        UPL[s] = jnp.where(valid(s), COT[s].astype(F32), 0.0).astype(BF)
         top, low_rows = pl.ds(0, HALF_TOK), pl.ds(HALF_TOK, HALF_TOK)
         send(("*UP", 0, s), UPL.at[s, top], UP.at[s, top], at(1 - c, z, x + 1, yl), guest)
         send(("*UP", 1, s), UPL.at[s, low_rows], UP.at[s, low_rows], at(1 - c, z, x + 3, yl), guest)
@@ -362,90 +360,111 @@
         add_into(4, lambda j: PT.at[z, j, yl, hv_b], lambda j: RBF.at[s, 0, j], lambda j: RBF.at[s, 1, j])
         owners(s, 1, hv_b)
 
-    def chosen(s, which):
-        return jnp.where(jnp.full((256, 256), index[s] % 2) == 0, MSG[s, 0, :, which].astype(F32),
-                         MSG[s, 1, :, which].astype(F32))
-
-    def U(s):
-        arrived(("*X", 0, s), RX.at[s, :, :, hv_a])
-        arrived(("*X", 1, s), RX.at[s, :, :, hv_b])
-        if s == 0:
-            inputs[2].wait()
-            for j in range(2):
-                step = jnp.full((8, 128), index[j]).astype(F32)
-                RATE[j] = 0.5 * math.sqrt(D / (TOK * 32)) * INV_ROOT * (1.0 + 0.5 * jnp.cos(jnp.pi * step / 1024.0))
+    def chosen(s, part):
+        return jnp.where(jnp.full((256, 256), index[s] % 2) == 0, MSG[s, 0, part].astype(F32),
+                         MSG[s, 1, part].astype(F32))
+
+    def U(s, part, hv):
+        arrived(("*X", part, s), RX.at[s, :, :, hv])
         if s == 1:
             for j in range(2):
-                arrived(("MSG", j, 0), MSG.at[0, j])
+                arrived(("MSG", j, part, 0), MSG.at[0, j, part])
+            message = chosen(0, part)
         for h in range(2):
-            cols = slice(h * 256, (h + 1) * 256)
-            grad = (RX[s, 0, h].astype(F32) + RX[s, 1, h].astype(F32)).T
+            mine, cols = slice(h * 128, (h + 1) * 128), slice(h * 256 + part * 128, h * 256 + (part + 1) * 128)
+            grad = (RX[s, 0, h, hv].astype(F32) + RX[s, 1, h, hv].astype(F32)).T
             block = NUM[:, cols] if s == 0 else X1[:, cols]
             kept = 0.5 * (block - RATE[s, 0:1, 0:1] * grad)
-            KB[s, :, cols] = kept.astype(BF)
-            if s == 0:
-                X1[:, cols] = kept + INB[:, cols]
-            else:
-                X1[:, cols] = kept + chosen(0, cols)
-        if s == 1:
-            result(X1, num_out.at[0])
-
-    def MS(s):
-        send(("MSG", 0, s), KB.at[s], MSG.at[s, 0], next1)
-        send(("MSG", 1, s), KB.at[s], MSG.at[s, 1], next2)
+            KB[s, part, :, mine] = kept.astype(BF)
+            X1[:, cols] = kept + (INB[:, cols] if s == 0 else message[:, mine])
+
+    def UA(s):
+        U(s, 0, hv_a)
+
+    def UB(s):
+        U(s, 1, hv_b)
+
+    def MS(s, part):
+        send(("MSG", 0, part, s), KB.at[s, part], MSG.at[s, 0, part], next1)
+        send(("MSG", 1, part, s), KB.at[s, part], MSG.at[s, 1, part], next2)
+
+    def MSA(s):
+        MS(s, 0)
+
+    def MSB(s):
+        MS(s, 1)
 
     def M(s):
+        result(X1, num_out.at[0])
         for j in range(2):
             arrived(("WT", j), WR.at[j])
         even0, even1 = index[0] % 2 == 0, index[1] % 2 == 0
         w_out[0] = 0.5 * weight_at(1) + 0.5 * jnp.where(even0, WR[0, 0, 0], WR[1, 0, 0])
         mw_out[0] = 0.5 * (0.5 * jnp.where(even1, WR[0, 0, 0], WR[1, 0, 0])
                            + jnp.where(even1, WR[0, 4, 0], WR[1, 4, 0]))
-        for j in range(2):
-            arrived(("MSG", j, 1), MSG.at[1, j])
-        for h in range(2):
-            cols = slice(h * 256, (h + 1) * 256)
-            INB[:, cols] = chosen(1, cols)
+        for part in range(2):
+            for j in range(2):
+                arrived(("MSG", j, part, 1), MSG.at[1, j, part])
+            message = chosen(1, part)
+            for h in range(2):
+                cols = slice(h * 256 + part * 128, h * 256 + (part + 1) * 128)
+                INB[:, cols] = message[:, h * 128:(h + 1) * 128]
         result(INB, inbox_out.at[0])
 
-    tasks = {
-        "AX": AX, "AY": AY, "AYz": AYz, "AYo": AYo, "AYn": pass_on("ZYy0", mate, z, yl, rows_b), "AY1": AY1,
-        "AZa": AZa, "AZb": AZb, "AZc": AZc,
-        "AZay": pass_on("ZYym", mate, zm, yl, rows_b), "AZby": pass_on("ZYyp", mate, zp, yl, rows_b),
-        "AZd": pass_on("YZfp", up_z, zm, yl, rows_a, "YZop"), "AZg": pass_on("YZfm", down_z, zp, my, rows_a, "YZmm"),
-        "FS0": pass_on("S0", sibling, z, yl, half(c)), "FS1": pass_on("S1", sibling, z, my, rows_a),
-        "FSa": pass_on("Sa", sibling, zm, yl, rows_b), "FSb": pass_on("Sb", sibling, zp, yl, rows_b),
-        "FSc": pass_on("Sc", sibling, z2, yl, rows_b), "FSd": pass_on("Sd", sibling, zm, yl, rows_a),
-        "FSe": pass_on("Se", sibling, zp, yl, rows_a, "YZom"), "FSf": pass_on("Sf", sibling, zm, my, rows_a, "YZmp"),
-        "FSg": pass_on("Sg", sibling, zp, my, rows_a), "FSh": pass_on("Sh", sibling, z2, yl, rows_a, "YZfp"),
-        "FSi": pass_on("Si", sibling, z2, my, rows_a, "YZfm"),
-        "FSya": pass_on("Sya", sibling, z0, my, rows_b, "ZYy0"), "FSyb": pass_on("Syb", sibling, zm, my, rows_b, "ZYym"),
-        "FSyc": pass_on("Syc", sibling, zp, my, rows_b, "ZYyp"), "FSyd": pass_on("Syd", sibling, z2, my, rows_b, "ZYy2"),
-        "V": V, "VR": VRet, "VM": VM, "UPs": UPs, "UT": UT, "T": T, "C": C, "D": Dd, "E": Ee, "AH": AH,
-        "Fmm": Fmm, "Fmo": Fmo, "Fpo": Fpo, "Fpm": Fpm, "Gmh": Gmh, "Gml": Gml, "Gpl": Gpl, "Gph": Gph,
-        "Hm": Hm, "Ho": Ho, "I": I, "J": J, "U": U, "MS": MS,
-    }
+    AYzp, AYzq = first_hop("ZYp", "ZYm", rows_b, own), first_hop("ZYp", "ZYm", rows_b, rest)
+    AYop, AYoq = first_hop("YZop", "YZom", rows_a, own), first_hop("YZop", "YZom", rows_a, rest)
+    AYnp, AYnq = to_mate("ZYy0", rows_b, own), to_mate("ZYy0", rows_b, rest)
+    AZay, AZby = pass_on("ZYym", mate, zm, yl, rows_b), pass_on("ZYyp", mate, zp, yl, rows_b)
+    AZd = pass_on("YZfp", up_z, zm, yl, rows_a, "YZop")
+    AZg = pass_on("YZfm", down_z, zp, my, rows_a, "YZmm")
+    FS0, FS1 = pass_on("S0", sibling, z, yl, half(c)), pass_on("S1", sibling, z, my, rows_a)
+    FSa, FSb = pass_on("Sa", sibling, zm, yl, rows_b), pass_on("Sb", sibling, zp, yl, rows_b)
+    FSc, FSd = pass_on("Sc", sibling, z2, yl, rows_b), pass_on("Sd", sibling, zm, yl, rows_a)
+    FSe, FSf = pass_on("Se", sibling, zp, yl, rows_a, "YZom"), pass_on("Sf", sibling, zm, my, rows_a, "YZmp")
+    FSg, FSh = pass_on("Sg", sibling, zp, my, rows_a), pass_on("Sh", sibling, z2, yl, rows_a, "YZfp")
+    FSi, FSya = pass_on("Si", sibling, z2, my, rows_a, "YZfm"), pass_on("Sya", sibling, z0, my, rows_b, "ZYy0")
+    FSyb, FSyc = pass_on("Syb", sibling, zm, my, rows_b, "ZYym"), pass_on("Syc", sibling, zp, my, rows_b, "ZYyp")
+    FSyd = pass_on("Syd", sibling, z2, my, rows_b, "ZYy2")
 
     barrier = pltpu.get_barrier_semaphore()
     others = [(lax.rem(rep + j, 4), fs) for j in (1, 2, 3)] + [mate, up_z, down_z]
     others += [at(core, z, x + j, yl) for core in (0, 1) for j in (1, 2, 3)]
     for other in others:
         pl.semaphore_signal(barrier, inc=1, device_id=other, device_id_type=MESH)
+    WT[...] = jnp.where(lax.broadcasted_iota(jnp.int32, (8, 128), 0) < 4, weight[0], inbox_wt[0])
+    for s in range(2):
+        step = jnp.full((8, 128), index[s]).astype(F32)
+        RATE[s] = 0.5 * math.sqrt(D / (TOK * 32)) * INV_ROOT * (1.0 + 0.5 * jnp.cos(jnp.pi * step / 1024.0))
+    inputs[0].wait()
+    project(0)
+    inputs[1].wait()
+    for s in range(2):
+        UPL[s] = jnp.where(valid(s), COT[s].astype(F32), 0.0).astype(BF)
+    inputs[2].wait()
     pl.semaphore_wait(barrier, len(others))
 
-    WT[...] = jnp.where(lax.broadcasted_iota(jnp.int32, (8, 128), 0) < 4, weight[0], inbox_wt[0])
     send(("WT", 0), WT, WR.at[0], next1)
     send(("WT", 1), WT, WR.at[1], next2)
-    started = set()
-    for entry in ORDER:
-        name, *numbers = entry.split(".")
-        if name == "M":
-            M(0)
-            continue
-        if name == "V" and ("V", numbers[0]) not in started:
-            started.add(("V", numbers[0]))
-            VC(0)
-        tasks[name](*map(int, numbers))
+    for task, *numbers in (
+        (UPs, 0), (AX, 0), (T, 0, 0), (AYp, 0), (AYop, 0), (AYzp, 0), (AY1p, 0), (T, 0, 1), (T, 0, 2), (AYq, 0),
+        (AYzq, 0), (AZa, 0), (T, 0, 3), (UT, 0), (AYoq, 0), (T, 0, 4), (AZb, 0), (C, 0, 0), (AZay, 0), (AY1, 0),
+        (FS1, 0), (C, 0, 1), (T, 0, 5), (C, 0, 2), (Dd, 0, 0), (T, 0, 6), (C, 0, 3), (T, 0, 7), (AH, 0), (T, 1, 0),
+        (UPs, 1), (AYnp, 0), (AZc, 0), (C, 0, 4), (Dd, 0, 1), (C, 0, 5), (Ee, 0, 0), (FS0, 0), (Fpm, 0), (T, 1, 1),
+        (Dd, 0, 2), (Fmm, 0), (Fpo, 0), (C, 0, 6), (Fmo, 0), (AYnq, 0), (FSyb, 0), (C, 0, 7), (Dd, 0, 3), (T, 1, 2),
+        (Ee, 0, 1), (Ee, 0, 2), (Gph, 0), (UT, 1), (Gml, 0), (Gpl, 0), (Gmh, 0), (Hm, 0), (AZd, 0), (FSd, 0),
+        (C, 1, 0), (AZg, 0), (C, 1, 1), (FSb, 0), (T, 1, 3), (AZby, 0), (Dd, 1, 0), (AH, 1), (Ho, 0), (Ee, 0, 3),
+        (J, 0), (C, 1, 2), (I, 0), (C, 1, 3), (FSc, 0), (FSyc, 0), (FSf, 0), (FSya, 0), (UB, 0), (Dd, 1, 1),
+        (UA, 0), (AX, 1), (Ee, 1, 0), (AYp, 1), (MSB, 0), (AYzp, 1), (Fpm, 1), (FSh, 0), (AYop, 1), (T, 1, 4),
+        (T, 1, 5), (Ee, 1, 1), (AYq, 1), (AYzq, 1), (Gpl, 1), (AYoq, 1), (FSe, 0), (C, 1, 4), (FSyd, 0), (T, 1, 6),
+        (FSa, 0), (T, 1, 7), (AY1p, 1), (AZb, 1), (AYnq, 1), (C, 1, 5), (AZa, 1), (AY1, 1), (FSa, 1), (Gph, 1),
+        (AZby, 1), (Fpo, 1), (FSb, 1), (AZay, 1), (FSg, 0), (V, 0, 2), (Dd, 1, 2), (C, 1, 6), (FSe, 1), (AYnp, 1),
+        (Fmm, 1), (C, 1, 7), (Dd, 1, 3), (Fmo, 1), (V, 0, 1), (AZd, 1), (FSd, 1), (AZc, 1), (FS1, 1), (Ee, 1, 2),
+        (FSc, 1), (FSf, 1), (FSyb, 1), (Hm, 1), (FS0, 1), (Gml, 1), (Gmh, 1), (MSA, 0), (AZg, 1), (FSi, 0),
+        (V, 0, 3), (Ee, 1, 3), (V, 0, 0), (FSg, 1), (VRet, 0), (V, 1, 2), (J, 1), (Ho, 1), (FSyd, 1), (FSyc, 1),
+        (FSya, 1), (I, 1), (V, 1, 1), (UB, 1), (MSB, 1), (FSh, 1), (FSi, 1), (UA, 1), (MSA, 1), (V, 1, 3), (VM, 0),
+        (V, 1, 0), (VRet, 1), (VM, 1), (M, 0),
+    ):
+        task(*numbers)
     for name in list(pending):
         sent(name)
     for copy in outputs:
@@ -498,8 +517,8 @@
             pltpu.VMEM((2, TOK, HV), BF),
             pltpu.VMEM((TOK, HV), F32),
             pltpu.VMEM((2, 256, HV), BF),
-            pltpu.VMEM((2, 256, HV), BF),
-            pltpu.VMEM((2, 2, 256, HV), BF),
+            pltpu.VMEM((2, 2, 256, 256), BF),
+            pltpu.VMEM((2, 2, 2, 256, 256), BF),
             pltpu.VMEM((256, HV), F32),
             pltpu.VMEM((8, 128), F32),
             pltpu.VMEM((2, 8, 128), F32),

time: 157 us -> 152 us (0.968)
  Pallas kernels: 154 us -> 149 us
    pallas_call x1, Pallas kernels: 150 us -> 145 us  [per_device(): pl.pallas_call(kernel, out_shape=(tokens, matrix, scalar, matrix, scalar)...]
where the time goes in v3:
time: 152 us; the launch traced here: 151 us
  Pallas kernels  149 us (98%)
  between operations  1.93 us (1%)
    pallas_call x1, Pallas kernels, per_device(): pl.pallas_call(kernel, out_shape=(tokens, matrix, scalar, matrix, scalar)...  145 us
    pallas_call x1, Pallas kernels, per_device(): pl.pallas_call(finish, out_shape=(tokens, matrix, matrix, scalar, scalar)...  4.24 us

profile of v3, /device:TPU:1, one launch (start us, length us, event | category | flops | bytes accessed | tf_op | source)
XLA Modules:
  0.0 151.3 jit_solution(18390747840966782402)
XLA Ops:
  1.9 145.2 %push_steps.1 = (bf16[2,1,384,512]{3,2,1,0:T(8,128)(2,1)}, f32[1,256,512]{2,1,0:T(8,128)}, f32[1]{0:T(128)}, f32[1,256,512]{2,1,0:T(8,128)}, f32[1]{0:T(128)}) custom-call(s32[2]{0:T(128)} %index.1, s32[2]{0:T(128)} %bitcast.1, f32[1]{0:T(128)S(6)} %copy.13.weight, f32[1]{0:T(128)S(6)} %copy.14.inbox_wt, bf16[2,1,384,8192]{3,2,1,0:T(8,128)(2,1)} %act.1, ...), custom_call_target="tpu_custom_call" | custom-call | flops 12884901888 | bytes 12582912 | tf_op jit(solution)/shard_map/push_steps/pallas_call | solution.py:495
  147.1 4.2 %finish.1 = (bf16[2,1,384,512]{3,2,1,0:T(8,128)(2,1)}, f32[1,256,512]{2,1,0:T(8,128)}, f32[1,256,512]{2,1,0:T(8,128)}, f32[1]{0:T(128)}, f32[1]{0:T(128)}) custom-call(bf16[2,1,384,512]{3,2,1,0:T(8,128)(2,1)} %get-tuple-element.15.val, f32[1,256,512]{2,1,0:T(8,128)} %get-tuple-element.16.num_out, f32[1,256,512]{2,1,0:T(8,128)} %get-tuple-element.17.inbox_out, ...), custom_call_target="tpu_custom_call" | custom-call | tf_op jit(solution)/shard_map/finish/pallas_call | solution.py:540

commit v4 on v3

--- a/solution.py
+++ b/solution.py
@@ -15,12 +15,11 @@
 HALF_TOK = TOK // 2
 ROUTE = 96
 HA = 128
-SUB = 1024
-
-
-def kernel(index, length, weight, inbox_wt, act, cot, num, inbox, val, num_out, w_out, inbox_out, mw_out,
+
+
+def kernel(index_at, length_at, weight_at_, inbox_wt_at, act, cot, num, inbox, val, num_out, w_out, inbox_out, mw_out,
            ACT, Z, PT, PS, RSIB, RAH, RAF, RAY, RBY, RBH, RBF, RX, UPL, UP, UPT, VB, VR, VACC,
-           ZS, KB, MSG, X1, WT, WR, COT, NUM, INB, RATE, ss, rs, io, credit):
+           ZS, KB, MSG, X1, WT, WR, COT, NUM, INB, RATE, index, length, weight, inbox_wt, wts0, wts1, ss, rs, io, credit):
     rep, fs = lax.axis_index("rep"), lax.axis_index("fsdp")
     yh, c = rep // 2, rep % 2
     z, x, yl = fs // 8, (fs // 2) % 4, fs % 2
@@ -36,11 +35,14 @@
     up_z, down_z = at(c, z + 1, x, yl), at(c, z + 3, x, yl)
     z0, zp, zm, z2 = z, lax.rem(z + 1, 4), lax.rem(z + 3, 4), lax.rem(z + 2, 4)
     chunk = (z2, zp, zm, z0)
+    parts = ((z2, 0), (z2, 1), (zp, 0), (zm, 0), (zp, 1), (zm, 1), (z0, 0), (z0, 1))
     next1, next2 = (lax.rem(rep + 1, 4), fs), (lax.rem(rep + 2, 4), fs)
 
     inputs = [pltpu.make_async_copy(*pair, io.at[i])
               for i, pair in enumerate([(num.at[0], NUM), (cot.at[:, 0], COT), (inbox.at[0], INB)])]
-    for copy in inputs:
+    numbers_in = [pltpu.make_async_copy(*pair, io.at[3 + i]) for i, pair in enumerate(
+        [(index_at, index), (length_at, length), (weight_at_, weight), (inbox_wt_at, inbox_wt)])]
+    for copy in numbers_in + inputs:
         copy.start()
     names, pending = {}, {}
 
@@ -84,6 +86,7 @@
     sib_b = pl.ds(pl.multiple_of((1 - c) * 128 + ROUTE, 16), 128 - ROUTE)
     hv_a, hv_b = pl.ds(0, HA), pl.ds(HA, 256 - HA)
     low, high, every = pl.ds(0, 2), pl.ds(2, 2), pl.ds(0, 4)
+    pairs = (low, high)
     own, rest = pl.ds(0, 1), pl.ds(1, 3)
 
     def weight_at(s):
@@ -208,7 +211,7 @@
     outputs = []
 
     def result(src, dst):
-        outputs.append(pltpu.make_async_copy(src, dst, io.at[3 + len(outputs)]))
+        outputs.append(pltpu.make_async_copy(src, dst, io.at[7 + len(outputs)]))
         outputs[-1].start()
 
     def UPs(s):
@@ -224,45 +227,44 @@
         other = UP[s, :, pl.ds(pl.multiple_of((1 - c) * 256, 256), 256)]
         UPT[s, 256:512] = other.astype(F32).T.astype(BF)
 
-    def columns_of(k):
-        return pl.ds(pl.multiple_of(chunk[k // 2] * 2048 + (k % 2) * SUB, SUB), SUB)
+    def columns_of(zz, xx):
+        return pl.ds(pl.multiple_of(zz * 2048 + lax.rem(xx, 4) * 512, 512), 512)
 
     def T(s, k):
-        cols = columns_of(k)
-        for j, to in ((0, x + 1), (1, x + 3)):
-            rows = pl.ds(j * HALF_TOK, HALF_TOK)
-            send(("*T", j, s, k), act.at[s, 0, rows, cols], ACT.at[s, rows, cols], at(1 - c, z, to, yl), guest)
-        local(("*T", 2, s, k), act.at[s, 0, :, cols], ACT.at[s, :, cols], home)
+        zz, h = parts[k]
+        for e in (2 * h, 2 * h + 1):
+            for j, to in ((0, x + 1), (1, x + 3)):
+                rows, cols = pl.ds(j * HALF_TOK, HALF_TOK), columns_of(zz, to + e)
+                send(("*T", 4 * j + e, s, k), act.at[s, 0, rows, cols], ACT.at[s, rows, cols],
+                     at(1 - c, z, to, yl), guest)
+            cols = columns_of(zz, x + e)
+            local(("*T", 8 + e, s, k), act.at[s, 0, :, cols], ACT.at[s, :, cols], home)
 
     def C(s, k):
-        zz = chunk[k // 2]
-        arrived(("*T", s, k), ACT.at[s, :, columns_of(k)])
-        if s == 1 and k % 2 == 0:
-            used = {0: ("Ahm", "Ahp", "Bhm", "Bhp"), 1: ("Afpo", "Afpm", "Bfpl", "Bfph"),
-                    2: ("Afmo", "Afmm", "Bfml", "Bfmh"), 3: ("Ay",)}[k // 2]
+        zz, h = parts[k]
+        arrived(("*T", s, k), ACT.at[s, :, pl.ds(0, 1024)])
+        if s == 1:
+            used = (("Ahm", "Bhm"), ("Ahp", "Bhp"), ("Afpl", "Bfpl"), ("Afml", "Bfml"), ("Afph", "Bfph"),
+                    ("Afmh", "Bfmh"), ("Ayl",), ("Ayh",))[k]
             for name in used:
                 sent((name, 0))
-            sent(("By", 0, k // 2))
+            sent(("By", 0, k))
             sent(("SIB", 0, k))
-            sent(("SIB", 0, k + 1))
-            if k == 6:
+            if k >= 6:
                 for part in range(2):
-                    for j in range(4):
+                    for j in (2 * h, 2 * h + 1):
                         sent(("*X", j, part, 0))
-            pl.semaphore_wait(credit.at[k // 2], 1)
+            pl.semaphore_wait(credit.at[k], 1)
 
         def body(j, carry):
-            cols = pl.ds(pl.multiple_of(zz * 2048 + j * 512, 512), 512)
-            block = jnp.dot(UPT[s], ACT[s, :, cols], preferred_element_type=F32).astype(BF)
+            block = jnp.dot(UPT[s], ACT[s, :, columns_of(zz, x + j)], preferred_element_type=F32).astype(BF)
             for yy in range(2):
                 PT[zz, j, yy] = block[0:256, yy * 256:(yy + 1) * 256]
                 PS[zz, j, yy] = block[256:512, yy * 256:(yy + 1) * 256]
             return carry
 
-        first = 2 * (k % 2)
-        lax.fori_loop(first, first + 2, body, 0)
-        pair = pl.ds(first, 2)
-        send(("SIB", s, k), PS.at[zz, pair], RSIB.at[zz, pair], sibling)
+        lax.fori_loop(2 * h, 2 * h + 2, body, 0)
+        send(("SIB", s, k), PS.at[zz, pairs[h]], RSIB.at[zz, pairs[h]], sibling)
 
     def add_into(count, target, *others):
         def body(j, carry):
@@ -274,41 +276,43 @@
         lax.fori_loop(0, count, body, 0)
 
     def Dd(s, k):
-        zz = chunk[k]
-        arrived(("SIB", s, 2 * k), RSIB.at[zz, low])
-        arrived(("SIB", s, 2 * k + 1), RSIB.at[zz, high])
-        add_into(8, lambda j: PT.at[zz, j // 2, j % 2], lambda j: RSIB.at[zz, j // 2, j % 2])
+        zz, h = parts[k]
+        arrived(("SIB", s, k), RSIB.at[zz, pairs[h]])
+        add_into(4, lambda j: PT.at[zz, 2 * h + j // 2, j % 2], lambda j: RSIB.at[zz, 2 * h + j // 2, j % 2])
         if s == 0:
             pl.semaphore_signal(credit.at[k], inc=1, device_id=sibling, device_id_type=MESH)
-        send(("By", s, k), PT.at[zz, :, my, hv_b], RBY.at[s, zz], mate)
-
-    def AH(s):
-        send(("Ahm", s), PT.at[z2, :, yl, hv_a], RAH.at[s, 0], down_z)
-        send(("Ahp", s), PT.at[z2, :, my, hv_a], RAH.at[s, 1], up_z)
+        send(("By", s, k), PT.at[zz, pairs[h], my, hv_b], RBY.at[s, zz, pairs[h]], mate)
 
     def Ee(s, k):
-        zz = chunk[k]
-        arrived(("By", s, k), RBY.at[s, zz])
-        add_into(4, lambda j: PT.at[zz, j, yl, hv_b], lambda j: RBY.at[s, zz, j])
+        zz, h = parts[k]
+        arrived(("By", s, k), RBY.at[s, zz, pairs[h]])
+        add_into(2, lambda j: PT.at[zz, 2 * h + j, yl, hv_b], lambda j: RBY.at[s, zz, 2 * h + j])
         if k == 0:
             send(("Bhm", s), PT.at[zz, low, yl, hv_b], RBH.at[s, 0], down_z)
+        if k == 1:
             send(("Bhp", s), PT.at[zz, high, yl, hv_b], RBH.at[s, 1], up_z)
 
-    def Fmm(s):
-        send(("Afmm", s), PT.at[zm, :, my, hv_a], RAF.at[s, 0, :, my], down_z)
-
-    def Fmo(s):
+    def AHm(s):
+        send(("Ahm", s), PT.at[z2, low, :, hv_a], RAH.at[s, 0], down_z)
+
+    def AHp(s):
+        send(("Ahp", s), PT.at[z2, high, :, hv_a], RAH.at[s, 1], up_z)
+
+    def Fml(s):
         arrived(("Ahm", s), RAH.at[s, 0])
-        add_into(4, lambda j: PT.at[zm, j, yl, hv_a], lambda j: RAH.at[s, 0, j])
-        send(("Afmo", s), PT.at[zm, :, yl, hv_a], RAF.at[s, 0, :, yl], down_z)
-
-    def Fpo(s):
-        send(("Afpo", s), PT.at[zp, :, yl, hv_a], RAF.at[s, 1, :, yl], up_z)
-
-    def Fpm(s):
+        add_into(4, lambda j: PT.at[zm, j // 2, j % 2, hv_a], lambda j: RAH.at[s, 0, j // 2, j % 2])
+        send(("Afml", s), PT.at[zm, low, :, hv_a], RAF.at[s, 0, low], down_z)
+
+    def Fmh(s):
+        send(("Afmh", s), PT.at[zm, high, :, hv_a], RAF.at[s, 0, high], down_z)
+
+    def Fpl(s):
+        send(("Afpl", s), PT.at[zp, low, :, hv_a], RAF.at[s, 1, low], up_z)
+
+    def Fph(s):
         arrived(("Ahp", s), RAH.at[s, 1])
-        add_into(4, lambda j: PT.at[zp, j, my, hv_a], lambda j: RAH.at[s, 1, j])
-        send(("Afpm", s), PT.at[zp, :, my, hv_a], RAF.at[s, 1, :, my], up_z)
+        add_into(4, lambda j: PT.at[zp, 2 + j // 2, j % 2, hv_a], lambda j: RAH.at[s, 1, j // 2, j % 2])
+        send(("Afph", s), PT.at[zp, high, :, hv_a], RAF.at[s, 1, high], up_z)
 
     def Gmh(s):
         send(("Bfmh", s), PT.at[zm, high, yl, hv_b], RBF.at[s, 0, high], down_z)
@@ -326,39 +330,54 @@
         add_into(2, lambda j: PT.at[zp, 2 + j, yl, hv_b], lambda j: RBH.at[s, 1, j])
         send(("Bfph", s), PT.at[zp, high, yl, hv_b], RBF.at[s, 1, high], up_z)
 
-    def H(s, yy, minus, plus):
-        arrived((minus, s), RAF.at[s, 0, :, yy])
-        arrived((plus, s), RAF.at[s, 1, :, yy])
-        add_into(4, lambda j: PT.at[z, j, yy, hv_a], lambda j: RAF.at[s, 0, j, yy], lambda j: RAF.at[s, 1, j, yy])
-
-    def Hm(s):
-        H(s, my, "Afmm", "Afpm")
-        send(("Ay", s), PT.at[z, :, my, hv_a], RAY.at[s], mate)
-
-    def Ho(s):
-        H(s, yl, "Afmo", "Afpo")
-
-    def owners(s, part, hv):
-        def piece(xx, i):
-            xx = lax.rem(xx, 4)
-            return PT.at[z, xx, yl, hv], RX.at[s, i, c, hv]
-
-        send(("*X", 0, part, s), *piece(x + 1, 1), at(q, z, x + 1, yl))
-        send(("*X", 1, part, s), *piece(x + 3, 0), at(q, z, x + 3, yl))
-        send(("*X", 2, part, s), *piece(x + 2, 1), at(q, z, x + 2, yl))
-        send(("*X", 3, part, s), *piece(x, 0), sibling, guest)
-        local(("*X", 4, part, s), *piece(x, 0), home)
-
-    def I(s):
-        arrived(("Ay", s), RAY.at[s])
-        add_into(4, lambda j: PT.at[z, j, yl, hv_a], lambda j: RAY.at[s, j])
-        owners(s, 0, hv_a)
-
-    def J(s):
-        for name, way, part in (("Bfml", 0, low), ("Bfmh", 0, high), ("Bfpl", 1, low), ("Bfph", 1, high)):
-            arrived((name, s), RBF.at[s, way, part])
-        add_into(4, lambda j: PT.at[z, j, yl, hv_b], lambda j: RBF.at[s, 0, j], lambda j: RBF.at[s, 1, j])
-        owners(s, 1, hv_b)
+    def H(s, h, minus, plus, name):
+        arrived((minus, s), RAF.at[s, 0, pairs[h]])
+        arrived((plus, s), RAF.at[s, 1, pairs[h]])
+        add_into(4, lambda j: PT.at[z, 2 * h + j // 2, j % 2, hv_a], lambda j: RAF.at[s, 0, 2 * h + j // 2, j % 2],
+                 lambda j: RAF.at[s, 1, 2 * h + j // 2, j % 2])
+        send((name, s), PT.at[z, pairs[h], my, hv_a], RAY.at[s, pairs[h]], mate)
+
+    def Hl(s):
+        H(s, 0, "Afml", "Afpl", "Ayl")
+
+    def Hh(s):
+        H(s, 1, "Afmh", "Afph", "Ayh")
+
+    def owners(s, part, hv, h):
+        def piece(place, i):
+            return PT.at[z, place, yl, hv], RX.at[s, i, c, hv]
+
+        if h == 0:
+            send(("*X", 1, part, s), *piece(1, 1), at(q, z, x + 1, yl))
+            send(("*X", 0, part, s), *piece(0, 0), sibling, guest)
+            local(("*X", 4, part, s), *piece(0, 0), home)
+        else:
+            send(("*X", 2, part, s), *piece(2, 1), at(q, z, x + 2, yl))
+            send(("*X", 3, part, s), *piece(3, 0), at(q, z, x + 3, yl))
+
+    def I(s, h, name):
+        arrived((name, s), RAY.at[s, pairs[h]])
+        add_into(2, lambda j: PT.at[z, 2 * h + j, yl, hv_a], lambda j: RAY.at[s, 2 * h + j])
+        owners(s, 0, hv_a, h)
+
+    def Il(s):
+        I(s, 0, "Ayl")
+
+    def Ih(s):
+        I(s, 1, "Ayh")
+
+    def J(s, h, minus, plus):
+        arrived((minus, s), RBF.at[s, 0, pairs[h]])
+        arrived((plus, s), RBF.at[s, 1, pairs[h]])
+        add_into(2, lambda j: PT.at[z, 2 * h + j, yl, hv_b], lambda j: RBF.at[s, 0, 2 * h + j],
+                 lambda j: RBF.at[s, 1, 2 * h + j])
+        owners(s, 1, hv_b, h)
+
+    def Jl(s):
+        J(s, 0, "Bfml", "Bfpl")
+
+    def Jh(s):
+        J(s, 1, "Bfmh", "Bfph")
 
     def chosen(s, part):
         return jnp.where(jnp.full((256, 256), index[s] % 2) == 0, MSG[s, 0, part].astype(F32),
@@ -378,8 +397,20 @@
             KB[s, part, :, mine] = kept.astype(BF)
             X1[:, cols] = kept + (INB[:, cols] if s == 0 else message[:, mine])
 
+    def weights():
+        for j in range(2):
+            arrived(("WT", j), WR.at[j])
+        even0, even1 = index[0] % 2 == 0, index[1] % 2 == 0
+        wts0[0] = 0.5 * weight_at(1) + 0.5 * jnp.where(even0, WR[0, 0, 0], WR[1, 0, 0])
+        wts1[0] = 0.5 * (0.5 * jnp.where(even1, WR[0, 0, 0], WR[1, 0, 0])
+                           + jnp.where(even1, WR[0, 4, 0], WR[1, 4, 0]))
+        result(wts0, w_out)
+        result(wts1, mw_out)
+
     def UA(s):
         U(s, 0, hv_a)
+        if s == 0:
+            weights()
 
     def UB(s):
         U(s, 1, hv_b)
@@ -396,12 +427,6 @@
 
     def M(s):
         result(X1, num_out.at[0])
-        for j in range(2):
-            arrived(("WT", j), WR.at[j])
-        even0, even1 = index[0] % 2 == 0, index[1] % 2 == 0
-        w_out[0] = 0.5 * weight_at(1) + 0.5 * jnp.where(even0, WR[0, 0, 0], WR[1, 0, 0])
-        mw_out[0] = 0.5 * (0.5 * jnp.where(even1, WR[0, 0, 0], WR[1, 0, 0])
-                           + jnp.where(even1, WR[0, 4, 0], WR[1, 4, 0]))
         for part in range(2):
             for j in range(2):
                 arrived(("MSG", j, part, 1), MSG.at[1, j, part])
@@ -431,6 +456,8 @@
     others += [at(core, z, x + j, yl) for core in (0, 1) for j in (1, 2, 3)]
     for other in others:
         pl.semaphore_signal(barrier, inc=1, device_id=other, device_id_type=MESH)
+    for copy in numbers_in:
+        copy.wait()
     WT[...] = jnp.where(lax.broadcasted_iota(jnp.int32, (8, 128), 0) < 4, weight[0], inbox_wt[0])
     for s in range(2):
         step = jnp.full((8, 128), index[s]).astype(F32)
@@ -446,23 +473,25 @@
     send(("WT", 0), WT, WR.at[0], next1)
     send(("WT", 1), WT, WR.at[1], next2)
     for task, *numbers in (
-        (UPs, 0), (AX, 0), (T, 0, 0), (AYp, 0), (AYop, 0), (AYzp, 0), (AY1p, 0), (T, 0, 1), (T, 0, 2), (AYq, 0),
-        (AYzq, 0), (AZa, 0), (T, 0, 3), (UT, 0), (AYoq, 0), (T, 0, 4), (AZb, 0), (C, 0, 0), (AZay, 0), (AY1, 0),
-        (FS1, 0), (C, 0, 1), (T, 0, 5), (C, 0, 2), (Dd, 0, 0), (T, 0, 6), (C, 0, 3), (T, 0, 7), (AH, 0), (T, 1, 0),
-        (UPs, 1), (AYnp, 0), (AZc, 0), (C, 0, 4), (Dd, 0, 1), (C, 0, 5), (Ee, 0, 0), (FS0, 0), (Fpm, 0), (T, 1, 1),
-        (Dd, 0, 2), (Fmm, 0), (Fpo, 0), (C, 0, 6), (Fmo, 0), (AYnq, 0), (FSyb, 0), (C, 0, 7), (Dd, 0, 3), (T, 1, 2),
-        (Ee, 0, 1), (Ee, 0, 2), (Gph, 0), (UT, 1), (Gml, 0), (Gpl, 0), (Gmh, 0), (Hm, 0), (AZd, 0), (FSd, 0),
-        (C, 1, 0), (AZg, 0), (C, 1, 1), (FSb, 0), (T, 1, 3), (AZby, 0), (Dd, 1, 0), (AH, 1), (Ho, 0), (Ee, 0, 3),
-        (J, 0), (C, 1, 2), (I, 0), (C, 1, 3), (FSc, 0), (FSyc, 0), (FSf, 0), (FSya, 0), (UB, 0), (Dd, 1, 1),
-        (UA, 0), (AX, 1), (Ee, 1, 0), (AYp, 1), (MSB, 0), (AYzp, 1), (Fpm, 1), (FSh, 0), (AYop, 1), (T, 1, 4),
-        (T, 1, 5), (Ee, 1, 1), (AYq, 1), (AYzq, 1), (Gpl, 1), (AYoq, 1), (FSe, 0), (C, 1, 4), (FSyd, 0), (T, 1, 6),
-        (FSa, 0), (T, 1, 7), (AY1p, 1), (AZb, 1), (AYnq, 1), (C, 1, 5), (AZa, 1), (AY1, 1), (FSa, 1), (Gph, 1),
-        (AZby, 1), (Fpo, 1), (FSb, 1), (AZay, 1), (FSg, 0), (V, 0, 2), (Dd, 1, 2), (C, 1, 6), (FSe, 1), (AYnp, 1),
-        (Fmm, 1), (C, 1, 7), (Dd, 1, 3), (Fmo, 1), (V, 0, 1), (AZd, 1), (FSd, 1), (AZc, 1), (FS1, 1), (Ee, 1, 2),
-        (FSc, 1), (FSf, 1), (FSyb, 1), (Hm, 1), (FS0, 1), (Gml, 1), (Gmh, 1), (MSA, 0), (AZg, 1), (FSi, 0),
-        (V, 0, 3), (Ee, 1, 3), (V, 0, 0), (FSg, 1), (VRet, 0), (V, 1, 2), (J, 1), (Ho, 1), (FSyd, 1), (FSyc, 1),
-        (FSya, 1), (I, 1), (V, 1, 1), (UB, 1), (MSB, 1), (FSh, 1), (FSi, 1), (UA, 1), (MSA, 1), (V, 1, 3), (VM, 0),
-        (V, 1, 0), (VRet, 1), (VM, 1), (M, 0),
+        (AX, 0), (UPs, 0), (AYp, 0), (T, 0, 0), (AYop, 0), (AYzp, 0), (AY1p, 0), (AYq, 0), (AYzq, 0), (T, 0, 1),
+        (AYoq, 0), (T, 0, 2), (UT, 0), (T, 0, 3), (AZa, 0), (AYnp, 0), (AY1, 0), (C, 0, 0), (AYnq, 0), (T, 0, 4),
+        (C, 0, 1), (AZb, 0), (AZay, 0), (Dd, 0, 0), (AHm, 0), (AZby, 0), (Dd, 0, 1), (T, 0, 5), (AHp, 0), (FSa, 0),
+        (T, 0, 6), (C, 0, 2), (Ee, 0, 0), (AZg, 0), (T, 0, 7), (C, 0, 3), (UPs, 1), (AZd, 0), (Dd, 0, 2), (C, 0, 4),
+        (FSf, 0), (FS1, 0), (AZc, 0), (T, 1, 0), (C, 0, 5), (T, 1, 1), (Ee, 0, 2), (Ee, 0, 1), (FSg, 0), (T, 1, 2),
+        (Dd, 0, 3), (Dd, 0, 4), (Fpl, 0), (Fml, 0), (Dd, 0, 5), (T, 1, 3), (C, 0, 6), (C, 0, 7), (Dd, 0, 6),
+        (Ee, 0, 4), (Fph, 0), (FSyb, 0), (FSyc, 0), (Fmh, 0), (Gpl, 0), (Dd, 0, 7), (FSb, 0), (UT, 1), (C, 1, 0),
+        (Hl, 0), (Ee, 0, 3), (Ee, 0, 5), (Gph, 0), (T, 1, 4), (Gmh, 0), (FSya, 0), (C, 1, 1), (FSh, 0), (Dd, 1, 0),
+        (FSe, 0), (Gml, 0), (Hh, 0), (AHm, 1), (Dd, 1, 1), (AHp, 1), (C, 1, 2), (C, 1, 3), (T, 1, 5), (Dd, 1, 2),
+        (Ee, 0, 6), (FSc, 0), (Fpl, 1), (Ee, 0, 7), (Ih, 0), (Ee, 1, 0), (C, 1, 4), (Dd, 1, 3), (FSd, 0),
+        (Ee, 1, 1), (Fml, 1), (Il, 0), (Jl, 0), (Jh, 0), (Dd, 1, 4), (C, 1, 5), (T, 1, 6), (FS0, 0), (Fph, 1),
+        (Ee, 1, 3), (UA, 0), (MSA, 0), (Gml, 1), (UB, 0), (Dd, 1, 5), (Fmh, 1), (AX, 1), (Ee, 1, 4), (Ee, 1, 2),
+        (Gph, 1), (AYp, 1), (AYzp, 1), (AYop, 1), (MSB, 0), (T, 1, 7), (FSi, 0), (Gpl, 1), (AY1p, 1), (AYq, 1),
+        (AYzq, 1), (C, 1, 6), (Ee, 1, 5), (FS0, 1), (AYoq, 1), (AYnq, 1), (FSyd, 0), (AYnp, 1), (V, 0, 2),
+        (C, 1, 7), (Dd, 1, 6), (Dd, 1, 7), (AY1, 1), (Gmh, 1), (FSya, 1), (V, 0, 3), (AZa, 1), (Hh, 1), (AZb, 1),
+        (AZby, 1), (V, 0, 1), (AZd, 1), (FSb, 1), (V, 0, 0), (VRet, 0), (FSe, 1), (FS1, 1), (AZg, 1), (Ee, 1, 7),
+        (Hl, 1), (Ee, 1, 6), (AZay, 1), (Jh, 1), (FSg, 1), (Jl, 1), (FSyc, 1), (FSf, 1), (AZc, 1), (Ih, 1),
+        (V, 1, 3), (FSa, 1), (Il, 1), (V, 1, 1), (FSc, 1), (FSd, 1), (FSyb, 1), (VM, 0), (UB, 1), (MSB, 1),
+        (FSh, 1), (FSi, 1), (UA, 1), (FSyd, 1), (V, 1, 2), (MSA, 1), (V, 1, 0), (VRet, 1), (VM, 1), (M, 0),
     ):
         task(*numbers)
     for name in list(pending):
@@ -471,14 +500,12 @@
         copy.wait()
 
 
-def finish(val, num_out, inbox_out, w_out, mw_out, val_to, num_to, inbox_to, w_to, mw_to, VAL, NUM, INB, sem):
-    trips = [(val, VAL, val_to), (num_out, NUM, num_to), (inbox_out, INB, inbox_to)]
+def finish(val, num_out, inbox_out, w_out, mw_out, val_to, num_to, inbox_to, w_to, mw_to, VAL, NUM, INB, W, MW, sem):
+    trips = [(num_out, NUM, num_to), (inbox_out, INB, inbox_to), (val, VAL, val_to), (w_out, W, w_to), (mw_out, MW, mw_to)]
     loads = [pltpu.make_async_copy(src, stop, sem.at[i]) for i, (src, stop, dst) in enumerate(trips)]
-    stores = [pltpu.make_async_copy(stop, dst, sem.at[3 + i]) for i, (src, stop, dst) in enumerate(trips)]
+    stores = [pltpu.make_async_copy(stop, dst, sem.at[5 + i]) for i, (src, stop, dst) in enumerate(trips)]
     for copy in loads:
         copy.start()
-    w_to[0] = w_out[0]
-    mw_to[0] = mw_out[0]
     for load, store in zip(loads, stores):
         load.wait()
         store.start()
@@ -487,7 +514,7 @@
 
 
 def per_device(activations, cotangent, numerator, weight, inbox_num, inbox_wt, lengths, step_index):
-    smem, hbm = (pl.BlockSpec(memory_space=m) for m in (pltpu.SMEM, pl.ANY))
+    hbm = pl.BlockSpec(memory_space=pl.ANY)
     hb = 256 - HA
     matrix = jax.ShapeDtypeStruct((1, 256, HV), F32)
     scalar = jax.ShapeDtypeStruct((1,), F32)
@@ -495,15 +522,15 @@
     values, num_out, w_out, inbox_out, mw_out = pl.pallas_call(
         kernel,
         out_shape=(tokens, matrix, scalar, matrix, scalar),
-        in_specs=[smem] * 4 + [hbm] * 4,
-        out_specs=(hbm, hbm, smem, hbm, smem),
+        in_specs=[hbm] * 8,
+        out_specs=(hbm,) * 5,
         scratch_shapes=[
             pltpu.VMEM((2, TOK, D), BF),
             pltpu.VMEM((2, 4, 4, 2, 256, HV), BF),
             pltpu.VMEM((4, 4, 2, 256, 256), BF),
             pltpu.VMEM((4, 4, 2, 256, 256), BF),
             pltpu.VMEM((4, 4, 2, 256, 256), BF),
-            pltpu.VMEM((2, 2, 4, HA, 256), BF),
+            pltpu.VMEM((2, 2, 2, 2, HA, 256), BF),
             pltpu.VMEM((2, 2, 4, 2, HA, 256), BF),
             pltpu.VMEM((2, 4, HA, 256), BF),
             pltpu.VMEM((2, 4, 4, hb, 256), BF),
@@ -526,10 +553,16 @@
             pltpu.VMEM((256, HV), F32),
             pltpu.VMEM((256, HV), F32),
             pltpu.VMEM((2, 8, 128), F32),
-            pltpu.SemaphoreType.DMA((256,)),
-            pltpu.SemaphoreType.DMA((256,)),
-            pltpu.SemaphoreType.DMA((8,)),
-            pltpu.SemaphoreType.REGULAR((4,)),
+            pltpu.SMEM((2,), jnp.int32),
+            pltpu.SMEM((2,), jnp.int32),
+            pltpu.SMEM((1,), F32),
+            pltpu.SMEM((1,), F32),
+            pltpu.SMEM((1,), F32),
+            pltpu.SMEM((1,), F32),
+            pltpu.SemaphoreType.DMA((320,)),
+            pltpu.SemaphoreType.DMA((320,)),
+            pltpu.SemaphoreType.DMA((16,)),
+            pltpu.SemaphoreType.REGULAR((8,)),
         ],
         compiler_params=pltpu.CompilerParams(
             collective_id=0, has_side_effects=True, vmem_limit_bytes=63 * 2**20
@@ -540,13 +573,15 @@
     values, num_out, inbox_out, w_out, mw_out = pl.pallas_call(
         finish,
         out_shape=(tokens, matrix, matrix, scalar, scalar),
-        in_specs=[hbm] * 3 + [smem] * 2,
-        out_specs=(hbm,) * 3 + (smem,) * 2,
+        in_specs=[hbm] * 5,
+        out_specs=(hbm,) * 5,
         scratch_shapes=[
             pltpu.VMEM((2, 1, TOK, HV), BF),
             pltpu.VMEM((1, 256, HV), F32),
             pltpu.VMEM((1, 256, HV), F32),
-            pltpu.SemaphoreType.DMA((6,)),
+            pltpu.SMEM((1,), F32),
+            pltpu.SMEM((1,), F32),
+            pltpu.SemaphoreType.DMA((10,)),
         ],
         name="finish",
     )(values, num_out, inbox_out, w_out, mw_out)

time: 152 us -> 150 us (0.987)
  Pallas kernels: 149 us -> 147 us
where the time goes in v4:
time: 150 us; the launch traced here: 149 us
  Pallas kernels  147 us (98%)
  between operations  1.93 us (1%)
    pallas_call x1, Pallas kernels, per_device(): pl.pallas_call(kernel, out_shape=(tokens, matrix, scalar, matrix, scalar)...  144 us
    pallas_call x1, Pallas kernels, per_device(): pl.pallas_call(finish, out_shape=(tokens, matrix, matrix, scalar, scalar)...  3.74 us

profile of v4, /device:TPU:1, one launch (start us, length us, event | category | flops | bytes accessed | tf_op | source)
XLA Modules:
  0.0 149.4 jit_solution(16870962991596735948)
XLA Ops:
  1.9 143.7 %push_steps.1 = (bf16[2,1,384,512]{3,2,1,0:T(8,128)(2,1)}, f32[1,256,512]{2,1,0:T(8,128)}, f32[1]{0:T(128)}, f32[1,256,512]{2,1,0:T(8,128)}, f32[1]{0:T(128)}) custom-call(s32[2]{0:T(128)} %index_at.1, s32[2]{0:T(128)} %bitcast.1, f32[1]{0:T(128)S(6)} %copy.13.weight_at_, f32[1]{0:T(128)S(6)} %copy.14.inbox_wt_at, bf16[2,1,384,8192]{3,2,1,0:T(8,128)(2,1)} %act.1, ...), custom_call_target="tpu_custom_call" | custom-call | flops 12884901888 | bytes 12582912 | tf_op jit(solution)/shard_map/push_steps/pallas_call | solution.py:522
  145.7 3.7 %finish.1 = (bf16[2,1,384,512]{3,2,1,0:T(8,128)(2,1)}, f32[1,256,512]{2,1,0:T(8,128)}, f32[1,256,512]{2,1,0:T(8,128)}, f32[1]{0:T(128)}, f32[1]{0:T(128)}) custom-call(bf16[2,1,384,512]{3,2,1,0:T(8,128)(2,1)} %get-tuple-element.15.val, f32[1,256,512]{2,1,0:T(8,128)} %get-tuple-element.16.num_out, f32[1,256,512]{2,1,0:T(8,128)} %get-tuple-element.17.inbox_out, ...), custom_call_target="tpu_custom_call" | custom-call | tf_op jit(solution)/shard_map/finish/pallas_call | solution.py:573

commit v5 on v4

--- a/solution.py
+++ b/solution.py
@@ -501,9 +501,10 @@
 
 
 def finish(val, num_out, inbox_out, w_out, mw_out, val_to, num_to, inbox_to, w_to, mw_to, VAL, NUM, INB, W, MW, sem):
-    trips = [(num_out, NUM, num_to), (inbox_out, INB, inbox_to), (val, VAL, val_to), (w_out, W, w_to), (mw_out, MW, mw_to)]
+    trips = [(val.at[s], VAL.at[s], val_to.at[s]) for s in range(2)]
+    trips += [(num_out, NUM, num_to), (inbox_out, INB, inbox_to), (w_out, W, w_to), (mw_out, MW, mw_to)]
     loads = [pltpu.make_async_copy(src, stop, sem.at[i]) for i, (src, stop, dst) in enumerate(trips)]
-    stores = [pltpu.make_async_copy(stop, dst, sem.at[5 + i]) for i, (src, stop, dst) in enumerate(trips)]
+    stores = [pltpu.make_async_copy(stop, dst, sem.at[6 + i]) for i, (src, stop, dst) in enumerate(trips)]
     for copy in loads:
         copy.start()
     for load, store in zip(loads, stores):
@@ -581,7 +582,7 @@
             pltpu.VMEM((1, 256, HV), F32),
             pltpu.SMEM((1,), F32),
             pltpu.SMEM((1,), F32),
-            pltpu.SemaphoreType.DMA((10,)),
+            pltpu.SemaphoreType.DMA((12,)),
         ],
         name="finish",
     )(values, num_out, inbox_out, w_out, mw_out)

time: 150 us -> 150 us (level)
  no operation moved by 1% of the time
where the time goes in v5:
time: 150 us; the launch traced here: 149 us
  Pallas kernels  147 us (98%)
  between operations  1.93 us (1%)
    pallas_call x1, Pallas kernels, per_device(): pl.pallas_call(kernel, out_shape=(tokens, matrix, scalar, matrix, scalar)...  144 us
    pallas_call x1, Pallas kernels, per_device(): pl.pallas_call(finish, out_shape=(tokens, matrix, matrix, scalar, scalar)...  3.67 us

profile of v5, /device:TPU:1, one launch (start us, length us, event | category | flops | bytes accessed | tf_op | source)
XLA Modules:
  0.0 149.3 jit_solution(13989045638273937882)
XLA Ops:
  1.9 143.7 %push_steps.1 = (bf16[2,1,384,512]{3,2,1,0:T(8,128)(2,1)}, f32[1,256,512]{2,1,0:T(8,128)}, f32[1]{0:T(128)}, f32[1,256,512]{2,1,0:T(8,128)}, f32[1]{0:T(128)}) custom-call(s32[2]{0:T(128)} %index_at.1, s32[2]{0:T(128)} %bitcast.1, f32[1]{0:T(128)S(6)} %copy.13.weight_at_, f32[1]{0:T(128)S(6)} %copy.14.inbox_wt_at, bf16[2,1,384,8192]{3,2,1,0:T(8,128)(2,1)} %act.1, ...), custom_call_target="tpu_custom_call" | custom-call | flops 12884901888 | bytes 12582912 | tf_op jit(solution)/shard_map/push_steps/pallas_call | solution.py:523
  145.7 3.7 %finish.1 = (bf16[2,1,384,512]{3,2,1,0:T(8,128)(2,1)}, f32[1,256,512]{2,1,0:T(8,128)}, f32[1,256,512]{2,1,0:T(8,128)}, f32[1]{0:T(128)}, f32[1]{0:T(128)}) custom-call(bf16[2,1,384,512]{3,2,1,0:T(8,128)(2,1)} %get-tuple-element.15.val, f32[1,256,512]{2,1,0:T(8,128)} %get-tuple-element.16.num_out, f32[1,256,512]{2,1,0:T(8,128)} %get-tuple-element.17.inbox_out, ...), custom_call_target="tpu_custom_call" | custom-call | tf_op jit(solution)/shard_map/finish/pallas_call | solution.py:574
